TPU v7x, 512 devices: a whole 4x8x8 slice. The times are simulated.
512 devices in a mesh: lon: 32 (over z_lo, y, core), lat: 16 (over z_hi, x).
Axes of the slice: x: 4, y: 8, z: 8 (z_hi: 4, z_lo: 2; z = z_hi * 2 + z_lo), core: 2. Of those that a mesh axis runs over, the one named last changes fastest.
Arguments:
- latent: bfloat16 [2, 192, 1536, 512], P(None, 'lat', 'lon'), may hold values from -6 to 6
- w_qkv: bfloat16 [512, 1536], replicated, may hold values from -0.25 to 0.25
- w_out: bfloat16 [512, 512], replicated, may hold values from -0.25 to 0.25
- b_out: float32 [512], replicated, may hold values from -3 to 3
- norm_gain: float32 [512], replicated, may hold values from 0.25 to 1.75
- norm_shift: float32 [512], replicated, may hold values from -2 to 2
- earth_bias: bfloat16 [32, 8, 144, 144], P('lat'), may hold values from -4 to 324
Outputs:
- updated: bfloat16 [2, 192, 1536, 512], P(None, 'lat', 'lon')
All inputs are finite; a program needn't handle non-finite values.
Results may differ from a plain program's by a relative error of at most 0.011.
Values may be sent and summed in bfloat16 or wider, within the bound.
A program may use at most 128 MiB of HBM per device.

v0:
```python
import jax
import jax.numpy as jnp
from jax import lax
from jax.sharding import PartitionSpec as P

WLAT = 6
WLON = 12
SLAT = 3
SLON = 6
WT = 144


def shifted(shard, axis, by):
    size = lax.axis_size(axis)
    return lax.ppermute(shard, axis, [(i, (i + by) % size) for i in range(size)])


def forward_bands(tile):
    east = shifted(tile[:, :, :SLON], "lon", -1)
    widened = jnp.concatenate([tile[:, :, SLON:], east], 2)
    south = shifted(widened[:, :SLAT], "lat", -1)
    return jnp.concatenate([widened[:, SLAT:], south], 1)


def backward_bands(tile):
    north = shifted(tile[:, -SLAT:], "lat", 1)
    taller = jnp.concatenate([north, tile[:, :-SLAT]], 1)
    west = shifted(taller[:, :, -SLON:], "lon", 1)
    return jnp.concatenate([west, taller[:, :, :-SLON]], 2)


def to_windows(tile):
    lev, rows, cols, width = tile.shape
    blocks = tile.reshape(lev, rows // WLAT, WLAT, cols // WLON, WLON, width)
    blocks = blocks.transpose(1, 3, 0, 2, 4, 5)
    return blocks.reshape(rows // WLAT, cols // WLON, WT, width)


def from_windows(wins, lev, rows, cols):
    width = wins.shape[-1]
    blocks = wins.reshape(rows // WLAT, cols // WLON, lev, WLAT, WLON, width)
    blocks = blocks.transpose(2, 0, 3, 1, 4, 5)
    return blocks.reshape(lev, rows, cols, width)


def dense_map(values, matrix):
    lead = values.shape[:-1]
    mixed = jnp.dot(
        values.reshape(-1, values.shape[-1]), matrix, preferred_element_type=jnp.float32
    )
    return mixed.reshape(lead + (matrix.shape[1],))


def local(latent, w_qkv, w_out, b_out, norm_gain, norm_shift, earth_bias):
    lev, rows, cols, width = latent.shape
    heads = earth_bias.shape[1]
    head_dim = width // heads
    nwl = rows // WLAT
    nwo = cols // WLON
    qkv = dense_map(to_windows(forward_bands(latent)), w_qkv).astype(jnp.bfloat16)
    wins = qkv.reshape(nwl, nwo, WT, 3, heads, head_dim)
    query, keys, values = (wins[:, :, :, 0], wins[:, :, :, 1], wins[:, :, :, 2])
    scores = jnp.einsum("abqhe,abkhe->abhqk", query, keys, preferred_element_type=jnp.float32)
    scores = scores / jnp.sqrt(jnp.float32(head_dim)) + earth_bias.astype(jnp.float32)[:, None]
    is_last = lax.axis_index("lat") == lax.axis_size("lat") - 1
    latrow = jnp.arange(WT) // WLON % WLAT
    window_last = jnp.logical_and(jnp.arange(nwl) == nwl - 1, is_last)
    group = jnp.logical_and(window_last[:, None], (latrow >= WLAT - SLAT)[None, :])
    allowed = group[:, :, None] == group[:, None, :]
    scores = jnp.where(allowed[:, None, None], scores, jnp.float32(-1e30))
    probs = jax.nn.softmax(scores, axis=-1).astype(jnp.bfloat16)
    attended = jnp.einsum("abhqk,abkhe->abqhe", probs, values, preferred_element_type=jnp.float32)
    attended = attended.astype(jnp.bfloat16).reshape(nwl, nwo, WT, width)
    moved_back = backward_bands(from_windows(attended, lev, rows, cols))
    returned = (dense_map(moved_back, w_out) + b_out).astype(jnp.bfloat16)
    values_f = returned.astype(jnp.float32)
    mean = jnp.mean(values_f, axis=-1, keepdims=True)
    var = jnp.mean((values_f - mean) ** 2, axis=-1, keepdims=True)
    normed = (values_f - mean) / jnp.sqrt(var + 1e-05) * norm_gain + norm_shift
    return (latent.astype(jnp.float32) + normed).astype(jnp.bfloat16)


def solution(mesh):
    placed = (P(None, "lat", "lon", None), P(), P(), P(), P(), P(), P("lat", None, None, None))
    return jax.shard_map(
        local, mesh=mesh, in_specs=placed, out_specs=P(None, "lat", "lon", None), check_vma=False
    )
```

profile of v0, /device:TPU:1, one launch (start us, length us, event | category | flops | bytes accessed | tf_op | source)
XLA Modules:
  0.0 124.0 jit_solution(10856493942741976407)
XLA Ops:
  0.0 1.1 slice.34
  1.1 8.8 %collective-permute-start = (bf16[2,12,6,512]{3,2,1,0:T(8,128)(2,1)S(1)}, bf16[2,12,6,512]{3,2,1,0:T(8,128)(2,1)S(1)}, u32[]{:S(2)}, u32[]{:S(2)}) collective-permute-start(bf16[2,12,6,512]{3,2,1,0:T(8,128)(2,1)S(1)} %slice.34), channel_id=1, source_target_pairs={{0,496},{16,0},{32,16},{48,32},{64,48},{80,64},{96,80},{112,96},{1... | collective-permute-start | bytes 442376 | tf_op jit(solution)/shard_map/ppermute | solution.py:15
  9.9 1.8 %slice.33 = bf16[2,12,42,512]{3,2,1,0:T(8,128)(2,1)S(1)} slice(bf16[2,12,48,512]{3,2,1,0:T(8,128)(2,1)} %param.7), slice={[0:2], [0:12], [6:48], [0:512]} | slice | bytes 2064384 | tf_op jit(solution)/shard_map/slice | solution.py:20
  11.7 2.8 %copy.21 = f32[2,8,144,144]{2,3,1,0:T(8,128)} copy(bf16[2,8,144,144]{3,2,1,0:T(8,128)(2,1)} %param.13) | data formatting | bytes 1990656 | tf_op jit(solution)/shard_map/convert_element_type | solution.py:64
  14.7 7.5 %collective-permute-start.1 = (bf16[2,3,48,512]{3,2,1,0:T(8,128)(2,1)S(1)}, bf16[2,3,48,512]{3,2,1,0:T(8,128)(2,1)S(1)}, u32[]{:S(2)}, u32[]{:S(2)}) collective-permute-start(bf16[2,3,48,512]{3,2,1,0:T(8,128)(2,1)S(1)} %pad_maximum_fusion.1), channel_id=1, source_target_pairs={{0,15},{1,0},{2,1},{3,2},{4,3},{5,4},{6,5},{7,6},{8,7},{9,8},{10,9... | collective-permute-start | bytes 884744 | tf_op jit(solution)/shard_map/ppermute | solution.py:15
  22.4 10.7 %collective-permute-done.1 = bf16[2,3,48,512]{3,2,1,0:T(8,128)(2,1)S(1)} collective-permute-done((bf16[2,3,48,512]{3,2,1,0:T(8,128)(2,1)S(1)}, bf16[2,3,48,512]{3,2,1,0:T(8,128)(2,1)S(1)}, u32[]{:S(2)}, u32[]{:S(2)}) %collective-permute-start.1) | collective-permute-done | bytes 294944 | tf_op jit(solution)/shard_map/ppermute | solution.py:15
  33.2 1.2 copy.15
  35.1 3.8 %convolution_convert_fusion = bf16[2,4,144,1536]{3,2,1,0:T(8,128)(2,1)} fusion(bf16[512,1536]{1,0:T(8,128)(2,1)S(1)} %copy-done, bf16[2,4,144,512]{3,1,2,0:T(4,128)(2,1)S(1)} %bitcast.42), kind=kOutput, calls=%fused_computation.10 | convolution fusion | flops 1813708800 | bytes 6291456 | tf_op jit(solution)/shard_map/dot_general | solution.py:48
  38.9 9.5 %reshape.111 = bf16[2,4,144,3,8,64]{5,4,3,2,1,0:T(8,128)(2,1)} reshape(bf16[2,4,144,1536]{3,2,1,0:T(8,128)(2,1)} %convolution_convert_fusion) | data formatting | bytes 7077888 | tf_op jit(solution)/shard_map/reshape | solution.py:61
  48.4 6.1 %fusion.32 = (bf16[2,4,144,1,8,64]{5,4,3,2,1,0:T(8,128)(2,1)}, bf16[2,4,144,1,8,64]{5,4,3,2,1,0:T(8,128)(2,1)}, bf16[2,4,144,1,8,64]{5,4,3,2,1,0:T(8,128)(2,1)}) fusion(bf16[2,4,144,3,8,64]{5,4,3,2,1,0:T(8,128)(2,1)} %reshape.111), kind=kLoop, calls=%fused_computation.54 | loop fusion | bytes 7077888 | tf_op jit(solution)/shard_map/slice | solution.py:62
  54.6 4.5 %copy.30 = bf16[2,4,144,1,8,64]{2,5,4,1,0,3:T(8,128)(2,1)} copy(bf16[2,4,144,1,8,64]{5,4,3,2,1,0:T(8,128)(2,1)} %get-tuple-element.5) | data formatting | bytes 2359296
  59.0 4.5 %copy.31 = bf16[2,4,144,1,8,64]{2,5,4,1,0,3:T(8,128)(2,1)} copy(bf16[2,4,144,1,8,64]{5,4,3,2,1,0:T(8,128)(2,1)} %get-tuple-element.6) | data formatting | bytes 2359296
  63.5 4.5 %copy.32 = bf16[2,4,144,1,8,64]{2,5,4,1,0,3:T(8,128)(2,1)} copy(bf16[2,4,144,1,8,64]{5,4,3,2,1,0:T(8,128)(2,1)} %get-tuple-element.7) | data formatting | bytes 2359296
  68.0 3.8 %fusion.14 = f32[2,4,8,144,144]{3,4,2,1,0:T(8,128)S(1)} fusion(bf16[2,4,144,1,8,64]{2,5,4,1,0,3:T(8,128)(2,1)} %copy.32, bf16[2,4,144,1,8,64]{2,5,4,1,0,3:T(8,128)(2,1)} %copy.31), kind=kOutput, calls=%fused_computation.21 | convolution fusion | flops 169869312 | bytes 7667712 | tf_op jit(solution)/shard_map/abqhe,abkhe->abhqk/dot_general | solution.py:63
  71.9 5.3 %fusion.33 = (f32[2,4,8,144]{3,2,1,0:T(8,128)S(1)}, f32[2,4,8,144,144]{3,4,2,1,0:T(8,128)}) fusion(f32[2,4,8,144,144]{3,4,2,1,0:T(8,128)S(1)} %fusion.14, f32[2,8,144,144]{2,3,1,0:T(8,128)S(1)} %copy-done.3, pred[2,144,144]{1,2,0:T(8,128)(4,1)S(1)} %broadcast_compare_fusion), kind=kOutput, calls=%fused_computation.55 | output fusion | flops 10616975 | bytes 12022272 | tf_op jit(solution)/shard_map/sub | solution.py:71
  77.2 6.0 %convert_bitcast_fusion = bf16[2,4,144,8,64]{2,4,3,1,0:T(8,128)(2,1)} fusion(f32[2,4,8,144,144]{3,4,2,1,0:T(8,128)} %get-tuple-element.9, f32[2,4,8,144]{3,2,1,0:T(8,128)S(1)} %get-tuple-element.8, bf16[2,4,144,1,8,64]{2,5,4,1,0,3:T(8,128)(2,1)S(1)} %copy-done.4), kind=kOutput, calls=%fused_computation.25 | convolution fusion | flops 173113344 | bytes 7704576 | tf_op jit(solution)/shard_map/abhqk,abkhe->abqhe/dot_general | solution.py:72
  83.2 4.8 %copy.23 = bf16[2,4,144,8,64]{4,3,1,2,0:T(8,128)(2,1)} copy(bf16[2,4,144,8,64]{2,4,3,1,0:T(8,128)(2,1)} %convert_bitcast_fusion) | data formatting | bytes 2359296 | tf_op jit(solution)/shard_map/convert_element_type | solution.py:73
  88.0 3.6 %reshape_reshape.4 = bf16[2,4,2,6,12,512]{5,1,4,3,2,0:T(4,128)(2,1)S(1)} reshape(bf16[2,4,144,8,64]{4,3,1,2,0:T(8,128)(2,1)} %copy.23) | data formatting | bytes 2359296 | tf_op jit(solution)/shard_map/reshape;reshape | solution.py:41
  91.6 1.2 copy.24
  93.1 2.1 %collective-permute-start.2 = (bf16[2,3,48,512]{3,2,1,0:T(8,128)(2,1)S(1)}, bf16[2,3,48,512]{3,2,1,0:T(8,128)(2,1)S(1)}, u32[]{:S(2)}, u32[]{:S(2)}) collective-permute-start(bf16[2,3,48,512]{3,2,1,0:T(8,128)(2,1)S(1)} %copy.33), channel_id=1, source_target_pairs={{0,1},{1,2},{2,3},{3,4},{4,5},{5,6},{6,7},{7,8},{8,9},{9,10},{10,1... | collective-permute-start | bytes 884744 | tf_op jit(solution)/shard_map/ppermute | solution.py:15
  95.8 15.8 %collective-permute-done.2 = bf16[2,3,48,512]{3,2,1,0:T(8,128)(2,1)S(1)} collective-permute-done((bf16[2,3,48,512]{3,2,1,0:T(8,128)(2,1)S(1)}, bf16[2,3,48,512]{3,2,1,0:T(8,128)(2,1)S(1)}, u32[]{:S(2)}, u32[]{:S(2)}) %collective-permute-start.2) | collective-permute-done | bytes 294944 | tf_op jit(solution)/shard_map/ppermute | solution.py:15
  111.9 6.3 %collective-permute-start.3 = (bf16[2,12,6,512]{3,2,1,0:T(8,128)(2,1)S(1)}, bf16[2,12,6,512]{3,2,1,0:T(8,128)(2,1)S(1)}, u32[]{:S(2)}, u32[]{:S(2)}) collective-permute-start(bf16[2,12,6,512]{3,2,1,0:T(8,128)(2,1)S(1)} %slice.51), channel_id=1, source_target_pairs={{0,16},{16,32},{32,48},{48,64},{64,80},{80,96},{96,112},{112,128},... | collective-permute-start | bytes 442376 | tf_op jit(solution)/shard_map/ppermute | solution.py:15
  118.2 2.6 %collective-permute-done.3 = bf16[2,12,6,512]{3,2,1,0:T(8,128)(2,1)S(1)} collective-permute-done((bf16[2,12,6,512]{3,2,1,0:T(8,128)(2,1)S(1)}, bf16[2,12,6,512]{3,2,1,0:T(8,128)(2,1)S(1)}, u32[]{:S(2)}, u32[]{:S(2)}) %collective-permute-start.3) | collective-permute-done | bytes 147488 | tf_op jit(solution)/shard_map/ppermute | solution.py:15
  122.3 1.7 %fusion.13 = bf16[2,12,48,512]{3,2,1,0:T(8,128)(2,1)} fusion(bf16[2,12,48,512]{3,2,1,0:T(8,128)(2,1)S(1)} %get-tuple-element.11, bf16[2,12,48,512]{3,2,1,0:T(8,128)(2,1)S(1)} %copy-done.2, f32[512]{0:T(512)S(1)} %copy-done.5, f32[512]{0:T(512)S(1)} %copy-done.6, f32[2,12,48]{2,1,0:T(8,128)S(1)} %add_sqrt_fusion, f32[2,12,48]{2,1,0:T(8,128)S(1)} %broadcast_multiply_fusion), kind=kLoop, calls=%fused_computation.20 | loop fusion | flops 4718592 | bytes 3552256 | tf_op jit(solution)/shard_map/convert_element_type | solution.py:80
  (37 shorter events, 3.7 us)
Async XLA Ops:
  0.0 35.1 %copy-start = (bf16[512,1536]{1,0:T(8,128)(2,1)S(1)}, bf16[512,1536]{1,0:T(8,128)(2,1)}, u32[]{:S(2)}) copy-start(bf16[512,1536]{1,0:T(8,128)(2,1)} %param.8) | copy-start | bytes 4718596
  1.1 13.6 %collective-permute-start = (bf16[2,12,6,512]{3,2,1,0:T(8,128)(2,1)S(1)}, bf16[2,12,6,512]{3,2,1,0:T(8,128)(2,1)S(1)}, u32[]{:S(2)}, u32[]{:S(2)}) collective-permute-start(bf16[2,12,6,512]{3,2,1,0:T(8,128)(2,1)S(1)} %slice.34), channel_id=1, source_target_pairs={{0,496},{16,0},{32,16},{48,32},{64,48},{80,64},{96,80},{112,96},{1... | collective-permute-start | bytes 442376 | tf_op jit(solution)/shard_map/ppermute | solution.py:15
  14.7 18.5 %collective-permute-start.1 = (bf16[2,3,48,512]{3,2,1,0:T(8,128)(2,1)S(1)}, bf16[2,3,48,512]{3,2,1,0:T(8,128)(2,1)S(1)}, u32[]{:S(2)}, u32[]{:S(2)}) collective-permute-start(bf16[2,3,48,512]{3,2,1,0:T(8,128)(2,1)S(1)} %pad_maximum_fusion.1), channel_id=1, source_target_pairs={{0,15},{1,0},{2,1},{3,2},{4,3},{5,4},{6,5},{7,6},{8,7},{9,8},{10,9... | collective-permute-start | bytes 884744 | tf_op jit(solution)/shard_map/ppermute | solution.py:15
  68.0 3.8 %copy-start.3 = (f32[2,8,144,144]{2,3,1,0:T(8,128)S(1)}, f32[2,8,144,144]{2,3,1,0:T(8,128)}, u32[]{:S(2)}) copy-start(f32[2,8,144,144]{2,3,1,0:T(8,128)} %copy.21) | copy-start | bytes 3981316
  71.9 5.3 %copy-start.4 = (bf16[2,4,144,1,8,64]{2,5,4,1,0,3:T(8,128)(2,1)S(1)}, bf16[2,4,144,1,8,64]{2,5,4,1,0,3:T(8,128)(2,1)}, u32[]{:S(2)}) copy-start(bf16[2,4,144,1,8,64]{2,5,4,1,0,3:T(8,128)(2,1)} %copy.30) | copy-start | bytes 3538948
  93.0 27.7 %copy-start.7 = (bf16[512,512]{1,0:T(8,128)(2,1)S(1)}, bf16[512,512]{1,0:T(8,128)(2,1)}, u32[]{:S(2)}) copy-start(bf16[512,512]{1,0:T(8,128)(2,1)} %param.9) | copy-start | bytes 1572868
  93.1 27.7 %copy-start.8 = (f32[512]{0:T(512)S(1)}, f32[512]{0:T(512)}, u32[]{:S(2)}) copy-start(f32[512]{0:T(512)} %param.10) | copy-start | bytes 6148
  93.1 18.6 %collective-permute-start.2 = (bf16[2,3,48,512]{3,2,1,0:T(8,128)(2,1)S(1)}, bf16[2,3,48,512]{3,2,1,0:T(8,128)(2,1)S(1)}, u32[]{:S(2)}, u32[]{:S(2)}) collective-permute-start(bf16[2,3,48,512]{3,2,1,0:T(8,128)(2,1)S(1)} %copy.33), channel_id=1, source_target_pairs={{0,1},{1,2},{2,3},{3,4},{4,5},{5,6},{6,7},{7,8},{8,9},{9,10},{10,1... | collective-permute-start | bytes 884744 | tf_op jit(solution)/shard_map/ppermute | solution.py:15
  111.9 8.9 %collective-permute-start.3 = (bf16[2,12,6,512]{3,2,1,0:T(8,128)(2,1)S(1)}, bf16[2,12,6,512]{3,2,1,0:T(8,128)(2,1)S(1)}, u32[]{:S(2)}, u32[]{:S(2)}) collective-permute-start(bf16[2,12,6,512]{3,2,1,0:T(8,128)(2,1)S(1)} %slice.51), channel_id=1, source_target_pairs={{0,16},{16,32},{32,48},{48,64},{64,80},{80,96},{96,112},{112,128},... | collective-permute-start | bytes 442376 | tf_op jit(solution)/shard_map/ppermute | solution.py:15
  120.8 1.5 %copy-start.2 = (bf16[2,12,48,512]{3,2,1,0:T(8,128)(2,1)S(1)}, bf16[2,12,48,512]{3,2,1,0:T(8,128)(2,1)}, u32[]{:S(2)}) copy-start(bf16[2,12,48,512]{3,2,1,0:T(8,128)(2,1)} %param.7) | copy-start | bytes 3538948
  120.8 1.5 %copy-start.5 = (f32[512]{0:T(512)S(1)}, f32[512]{0:T(512)}, u32[]{:S(2)}) copy-start(f32[512]{0:T(512)} %param.12) | copy-start | bytes 6148
  120.8 1.5 %copy-start.6 = (f32[512]{0:T(512)S(1)}, f32[512]{0:T(512)}, u32[]{:S(2)}) copy-start(f32[512]{0:T(512)} %param.11) | copy-start | bytes 6148
  121.7 2.3 %copy-start.1 = (bf16[512,1536]{1,0:T(8,128)(2,1)S(1)}, bf16[512,1536]{1,0:T(8,128)(2,1)}, u32[]{:S(2)}) copy-start(bf16[512,1536]{1,0:T(8,128)(2,1)} %param.8) | copy-start | bytes 4718596
where the time goes:
time: 126 us; the launch traced here: 124 us
  local copies, waits for them, and re-layouts  47.4 us (38%)
  waiting for transfers between devices  29.2 us (23%)
  starting transfers between devices  24.6 us (20%)
  matrix products  14.5 us (12%)
  other arithmetic  8 us (6%)
    ppermute x4, waiting for transfers between devices, shifted(): lax.ppermute(shard, axis, [(i, (i + by) % size) for i in range(size)])  29.2 us
    ppermute x4, starting transfers between devices, shifted(): lax.ppermute(shard, axis, [(i, (i + by) % size) for i in range(size)])  24.6 us
    unnamed x23, local copies, waits for them, and re-layouts  13.6 us
    reshape x1, local copies, waits for them, and re-layouts, local(): wins = qkv.reshape(nwl, nwo, WT, 3, heads, head_dim)  9.53 us
    slice x1, local copies, waits for them, and re-layouts, local(): query, keys, values = (wins[:, :, :, 0], wins[:, :, :, 1], wins[:, :, :, 2])  6.14 us
    dot_general x1, matrix products, local(): jnp.einsum('abhqk,abkhe->abqhe', probs, values, preferred_element_type=jn...  6.04 us
    sub x1, other arithmetic, local(): probs = jax.nn.softmax(scores, axis=-1).astype(jnp.bfloat16)  5.29 us
    convert_element_type x1, local copies, waits for them, and re-layouts, local(): attended = attended.astype(jnp.bfloat16).reshape(nwl, nwo, WT, width)  4.75 us
  transfers between devices with their start and end apart: 4, of which 3 were waited for; matrix products, arithmetic and copies ran while one was open for 5% of the time, Pallas kernels for 0%

commit v1 on v0

v1 whole, which is shorter than its diff:
```python
import functools

import jax
import jax.numpy as jnp
from jax import lax
from jax.experimental import pallas as pl
from jax.experimental.pallas import tpu as pltpu
from jax.sharding import PartitionSpec as P

LEV = 2
WLAT = 6
WLON = 12
SLAT = 3
SLON = 6
WT = 144
HEADS = 8
D = 512
LT = 4
F32 = jnp.float32
BF16 = jnp.bfloat16
MESH = pl.DeviceIdType.MESH

(C_LAT_M, C_LAT_S, C_LAT_N, C_WQKV, C_WOUT, C_BIAS, C_OUT_M, C_OUT_S, C_OUT_N) = range(9)
(R_EM, R_ES, R_S0, R_S1, R_S2, R_COR, R_RM, R_RS, R_R0, R_R1, R_R2, R_RC, R_RD) = range(13)


def split_tiles(value):
    return [value[..., 128 * t : 128 * (t + 1)] for t in range(LT)]


def kernel(
    nlat, nlon,
    lat_h, wqkv_h, wout_h, b_out, gain, shift, bias_h, out_h,
    lat_v, wqkv, wout, bias_v, biasf, fx, pf, win_in, win_out, cmp_f,
    ehalo, shalo, chalo, s80, s48, r80, r48, out_v,
    lsem, ssem, rsem,
):
    ilat, ilon = lax.axis_index("lat"), lax.axis_index("lon")
    north = lax.rem(ilat + nlat - 1, nlat)
    south = lax.rem(ilat + 1, nlat)
    west = lax.rem(ilon + nlon - 1, nlon)
    east = lax.rem(ilon + 1, nlon)
    to_n = {"lat": north, "lon": ilon}
    to_s = {"lat": south, "lon": ilon}
    to_w = {"lat": ilat, "lon": west}
    to_e = {"lat": ilat, "lon": east}
    to_nw = {"lat": north, "lon": west}
    to_se = {"lat": south, "lon": east}

    barrier = pltpu.get_barrier_semaphore()
    for who in (to_n, to_s, to_w, to_e, to_nw, to_se):
        pl.semaphore_signal(barrier, inc=1, device_id=who, device_id_type=MESH)

    def local(src, dst, which):
        return pltpu.make_async_copy(src, dst, lsem.at[which])

    def remote(src, dst, which, who):
        return pltpu.make_async_remote_copy(
            src_ref=src, dst_ref=dst, send_sem=ssem.at[which], recv_sem=rsem.at[which],
            device_id=who, device_id_type=MESH,
        )

    loads = {
        C_LAT_M: local(lat_h.at[:, 3:9], lat_v.at[:, 3:9], C_LAT_M),
        C_WQKV: local(wqkv_h, wqkv, C_WQKV),
        C_BIAS: local(bias_h, bias_v, C_BIAS),
        C_WOUT: local(wout_h, wout, C_WOUT),
        C_LAT_S: local(lat_h.at[:, 9:12], lat_v.at[:, 9:12], C_LAT_S),
        C_LAT_N: local(lat_h.at[:, 0:3], lat_v.at[:, 0:3], C_LAT_N),
    }
    for copy in loads.values():
        copy.start()

    sends = {
        R_S0: remote(lat_h.at[:, 0:3, 0:16], shalo.at[0], R_S0, to_n),
        R_EM: remote(lat_h.at[:, 3:9, 0:16], ehalo.at[:, 0:6], R_EM, to_w),
        R_S1: remote(lat_h.at[:, 0:3, 16:32], shalo.at[1], R_S1, to_n),
        R_S2: remote(lat_h.at[:, 0:3, 32:48], shalo.at[2], R_S2, to_n),
        R_ES: remote(lat_h.at[:, 9:12, 0:16], ehalo.at[:, 6:9], R_ES, to_w),
        R_COR: remote(shalo.at[0], chalo, R_COR, to_w),
        R_RM: remote(s80.at[3], r80.at[3], R_RM, to_e),
        R_RS: remote(s48.at[0], r48.at[0], R_RS, to_e),
        R_R0: remote(s80.at[0], r80.at[0], R_R0, to_s),
        R_R1: remote(s80.at[1], r80.at[1], R_R1, to_s),
        R_R2: remote(s80.at[2], r80.at[2], R_R2, to_s),
        R_RC: remote(s48.at[1], r48.at[1], R_RC, to_s),
        R_RD: remote(s48.at[2], r48.at[2], R_RD, to_se),
    }
    pl.semaphore_wait(barrier, 6)
    for which in (R_S0, R_EM, R_S1, R_S2, R_ES):
        sends[which].start()

    loads[C_BIAS].wait()
    is_last = ilat == nlat - 1

    def south_half(axis):
        at = lax.broadcasted_iota(jnp.int32, (WT, WT), axis)
        return jnp.logical_or(jnp.logical_and(at >= 36, at < 72), at >= 108)

    apart = jnp.logical_and(south_half(0) != south_half(1), is_last)
    penalty = jnp.where(apart, F32(-1e30), F32(0.0))
    for r in range(2):
        for h in range(HEADS):
            value = bias_v[r, h].astype(F32)
            biasf[r, h // 2, WT * (h % 2) : WT * (h % 2 + 1), :] = value + penalty if r else value

    lane = lax.broadcasted_iota(jnp.int32, (1, 128), 1)
    first = lane < 64
    scale0 = jnp.where(first, F32(0.125), F32(0.0))
    scale1 = jnp.where(first, F32(0.0), F32(0.125))

    def spread(value, dst):
        for t, tile in enumerate(split_tiles(value)):
            dst[t][...] = tile.astype(F32)

    def attend(r, x):
        qkv = jnp.dot(x, wqkv[...], preferred_element_type=F32)
        parts = []
        for p in range(HEADS // 2):
            qf = qkv[:, 128 * p : 128 * (p + 1)]
            kp = qkv[:, D + 128 * p : D + 128 * (p + 1)].astype(BF16)
            vp = qkv[:, 2 * D + 128 * p : 2 * D + 128 * (p + 1)].astype(BF16)
            q2 = jnp.concatenate([(qf * scale0).astype(BF16), (qf * scale1).astype(BF16)], 0)
            s = lax.dot_general(q2, kp, (((1,), (1,)), ((), ())), preferred_element_type=F32)
            s = s + biasf[r, p]
            e = jnp.exp(s - jnp.max(s, axis=-1, keepdims=True)).astype(BF16)
            vx = jnp.concatenate([vp, jnp.ones((WT, 128), BF16)], 1)
            o = jnp.dot(e, vx, preferred_element_type=F32)
            num = jnp.where(first, o[:WT, :128], o[WT:, :128])
            den = jnp.where(first, o[:WT, 128:], o[WT:, 128:])
            parts.append((num / den).astype(BF16))
        att = jnp.concatenate(parts, 1)
        proj = jnp.dot(att, wout[...], preferred_element_type=F32) + b_out[...]
        return proj.astype(BF16).astype(F32)

    def compact(rows_of, dst, width, at):
        slot = cmp_f.at[at]
        for n, row in enumerate(rows_of):
            slot[:, width * n : width * (n + 1), :] = win_out[at, :, row : row + width, :]
        size = dst.shape[0]
        for t in range(LT):
            dst[:, 128 * t : 128 * (t + 1)] = slot[t, 0:size, :].astype(BF16)

    def window(r, b):
        at = b % 2
        for l in range(LEV):
            for i in range(WLAT):
                j = WLON * (WLAT * l + i)
                win_in[at, :, j : j + WLON, :] = fx[
                    :, l, WLAT * r + i, SLON + WLON * b : SLON + WLON * (b + 1), :
                ]
        x = jnp.concatenate([win_in[at, t].astype(BF16) for t in range(LT)], 1)
        proj = attend(r, x)
        for t, tile in enumerate(split_tiles(proj)):
            win_out[at, t] = tile
        own = WLON if b < 3 else SLON
        for l in range(LEV):
            for i in range(WLAT if r == 0 else SLAT):
                j = WLON * (WLAT * l + i)
                pf[:, l, 3 + WLAT * r + i, SLON + WLON * b : SLON + WLON * b + own, :] = win_out[
                    at, :, j : j + own, :
                ]
        at_row = lambda l, i: WLON * (WLAT * l + i)
        if r == 0 and b == 3:
            compact([at_row(l, i) + SLON for l in range(LEV) for i in range(WLAT)], s80.at[3], SLON, at)
            sends[R_RM].start()
        if r == 1 and b < 3:
            compact([at_row(l, i) for l in range(LEV) for i in range(SLAT, WLAT)], s80.at[b], WLON, at)
            sends[R_R0 + b].start()
        if r == 1 and b == 3:
            low = [(l, i) for l in range(LEV) for i in range(SLAT, WLAT)]
            compact([at_row(l, i) + SLON for l, i in low], s48.at[2], SLON, at)
            sends[R_RD].start()
            compact([at_row(l, i) for l, i in low], s48.at[1], SLON, at)
            sends[R_RC].start()
            high = [(l, i) for l in range(LEV) for i in range(SLAT)]
            compact([at_row(l, i) + SLON for l, i in high], s48.at[0], SLON, at)
            sends[R_RS].start()

    def unpack(src, width, at, places):
        slot = cmp_f.at[at]
        size = src.shape[0]
        for t in range(LT):
            slot[t, 0:size, :] = src[:, 128 * t : 128 * (t + 1)].astype(F32)
        for n, (l, row, col) in enumerate(places):
            pf[:, l, row, col : col + width, :] = slot[:, width * n : width * (n + 1), :]

    def finish(row0, row1):
        for l in range(LEV):
            for row in range(row0, row1):
                v = jnp.concatenate([pf[t, l, row] for t in range(LT)], 1)
                mean = jnp.mean(v, axis=-1, keepdims=True)
                d = v - mean
                var = jnp.mean(d * d, axis=-1, keepdims=True)
                normed = d * lax.rsqrt(var + F32(1e-5)) * gain[...] + shift[...]
                out_v[l, row] = (lat_v[l, row].astype(F32) + normed).astype(BF16)

    loads[C_LAT_M].wait()
    for l in range(LEV):
        for i in range(6):
            spread(lat_v[l, 3 + i], [fx.at[t, l, i, 0:48] for t in range(LT)])
    loads[C_WQKV].wait()
    loads[C_WOUT].wait()
    for b in range(3):
        window(0, b)
    sends[R_EM].wait_recv()
    for l in range(LEV):
        for i in range(6):
            spread(ehalo[l, i], [fx.at[t, l, i, 48:64] for t in range(LT)])
    window(0, 3)

    loads[C_LAT_S].wait()
    for l in range(LEV):
        for i in range(3):
            spread(lat_v[l, 9 + i], [fx.at[t, l, 6 + i, 0:48] for t in range(LT)])

    def take_south(p):
        for l in range(LEV):
            for i in range(3):
                spread(shalo[p, l, i], [fx.at[t, l, 9 + i, 16 * p : 16 * (p + 1)] for t in range(LT)])

    sends[R_S0].wait_recv()
    sends[R_COR].start()
    take_south(0)
    sends[R_S1].wait_recv()
    take_south(1)
    window(1, 0)
    window(1, 1)
    sends[R_S2].wait_recv()
    take_south(2)
    window(1, 2)
    sends[R_ES].wait_recv()
    sends[R_COR].wait_recv()
    for l in range(LEV):
        for i in range(3):
            spread(ehalo[l, 6 + i], [fx.at[t, l, 6 + i, 48:64] for t in range(LT)])
            spread(chalo[l, i], [fx.at[t, l, 9 + i, 48:64] for t in range(LT)])
    window(1, 3)

    sends[R_RM].wait_recv()
    unpack(r80.at[3], SLON, 0, [(l, 3 + i, 0) for l in range(LEV) for i in range(WLAT)])
    finish(3, 9)
    out_m = local(out_v.at[:, 3:9], out_h.at[:, 3:9], C_OUT_M)
    out_m.start()
    loads[C_LAT_N].wait()
    sends[R_RS].wait_recv()
    unpack(r48.at[0], SLON, 1, [(l, 9 + i, 0) for l in range(LEV) for i in range(SLAT)])
    finish(9, 12)
    out_s = local(out_v.at[:, 9:12], out_h.at[:, 9:12], C_OUT_S)
    out_s.start()
    for b in range(3):
        sends[R_R0 + b].wait_recv()
        unpack(
            r80.at[b], WLON, b % 2,
            [(l, i, SLON + WLON * b) for l in range(LEV) for i in range(SLAT)],
        )
    sends[R_RC].wait_recv()
    unpack(r48.at[1], SLON, 1, [(l, i, 42) for l in range(LEV) for i in range(SLAT)])
    sends[R_RD].wait_recv()
    unpack(r48.at[2], SLON, 0, [(l, i, 0) for l in range(LEV) for i in range(SLAT)])
    finish(0, 3)
    out_n = local(out_v.at[:, 0:3], out_h.at[:, 0:3], C_OUT_N)
    out_n.start()
    for copy in sends.values():
        copy.wait_send()
    out_m.wait()
    out_s.wait()
    out_n.wait()


def local_step(nlat, nlon, latent, w_qkv, w_out, b_out, norm_gain, norm_shift, earth_bias):
    hbm = pl.BlockSpec(memory_space=pl.ANY)
    vmem = pl.BlockSpec(memory_space=pltpu.VMEM)
    tile = latent.shape
    return pl.pallas_call(
        functools.partial(kernel, nlat, nlon),
        out_shape=jax.ShapeDtypeStruct(tile, BF16),
        in_specs=[hbm, hbm, hbm, vmem, vmem, vmem, hbm],
        out_specs=hbm,
        scratch_shapes=[
            pltpu.VMEM(tile, BF16),
            pltpu.VMEM((D, 3 * D), BF16),
            pltpu.VMEM((D, D), BF16),
            pltpu.VMEM((2, HEADS, WT, WT), BF16),
            pltpu.VMEM((2, HEADS // 2, 2 * WT, WT), F32),
            pltpu.VMEM((LT, LEV, 12, 64, 128), F32),
            pltpu.VMEM((LT, LEV, 12, 48, 128), F32),
            pltpu.VMEM((2, LT, WT, 128), F32),
            pltpu.VMEM((2, LT, WT, 128), F32),
            pltpu.VMEM((2, LT, 80, 128), F32),
            pltpu.VMEM((LEV, 9, 16, D), BF16),
            pltpu.VMEM((3, LEV, 3, 16, D), BF16),
            pltpu.VMEM((LEV, 3, 16, D), BF16),
            pltpu.VMEM((4, 80, D), BF16),
            pltpu.VMEM((3, 48, D), BF16),
            pltpu.VMEM((4, 80, D), BF16),
            pltpu.VMEM((3, 48, D), BF16),
            pltpu.VMEM(tile, BF16),
            pltpu.SemaphoreType.DMA((9,)),
            pltpu.SemaphoreType.DMA((13,)),
            pltpu.SemaphoreType.DMA((13,)),
        ],
        compiler_params=pltpu.CompilerParams(
            collective_id=0, has_side_effects=True, vmem_limit_bytes=48 * 1024 * 1024
        ),
        name="swin_window_attention",
    )(
        latent, w_qkv, w_out, b_out.reshape(1, D), norm_gain.reshape(1, D),
        norm_shift.reshape(1, D), earth_bias,
    )


def solution(mesh):
    placed = (P(None, "lat", "lon", None), P(), P(), P(), P(), P(), P("lat", None, None, None))
    step = functools.partial(local_step, mesh.shape["lat"], mesh.shape["lon"])
    return jax.shard_map(
        step, mesh=mesh, in_specs=placed, out_specs=P(None, "lat", "lon", None), check_vma=False
    )
```

time: 126 us -> 54.5 us (0.43)
  the two profiles are of different devices: /device:TPU:1 before, /device:TPU:56 now
where the time goes in v1:
time: 54.5 us; the launch traced here: 54.1 us
  Pallas kernels  46.1 us (85%)
  local copies, waits for them, and re-layouts  8.05 us (15%)
    pallas_call x1, Pallas kernels, local_step(): pl.pallas_call(functools.partial(kernel, nlat, nlon), out_shape=jax.Shape...  46.1 us
    unnamed x15, local copies, waits for them, and re-layouts  8.05 us

profile of v1, /device:TPU:56, one launch (start us, length us, event | category | flops | bytes accessed | tf_op | source)
XLA Modules:
  0.0 54.1 jit_solution(8691749770952342145)
XLA Ops:
  0.0 0.0 copy-start
  0.0 1.4 %copy-done = bf16[512,1536]{1,0:T(8,128)(2,1)S(1)} copy-done((bf16[512,1536]{1,0:T(8,128)(2,1)S(1)}, bf16[512,1536]{1,0:T(8,128)(2,1)}, u32[]{:S(2)}) %copy-start) | copy-done | bytes 1572888
  1.4 0.0 copy-start.1
  1.4 1.3 %copy-done.1 = bf16[2,12,48,512]{3,2,1,0:T(8,128)(2,1)S(1)} copy-done((bf16[2,12,48,512]{3,2,1,0:T(8,128)(2,1)S(1)}, bf16[2,12,48,512]{3,2,1,0:T(8,128)(2,1)}, u32[]{:S(2)}) %copy-start.1) | copy-done | bytes 1179672
  2.7 0.0 copy-start.2
  2.7 1.3 %copy-done.2 = bf16[2,8,144,144]{3,2,1,0:T(8,128)(2,1)S(1)} copy-done((bf16[2,8,144,144]{3,2,1,0:T(8,128)(2,1)S(1)}, bf16[2,8,144,144]{3,2,1,0:T(8,128)(2,1)}, u32[]{:S(2)}) %copy-start.2) | copy-done | bytes 663576
  4.0 0.0 copy-start.3
  4.0 1.0 %copy-done.3 = bf16[512,512]{1,0:T(8,128)(2,1)S(1)} copy-done((bf16[512,512]{1,0:T(8,128)(2,1)S(1)}, bf16[512,512]{1,0:T(8,128)(2,1)}, u32[]{:S(2)}) %copy-start.3) | copy-done | bytes 524312
  5.0 0.0 copy-start.4
  5.0 0.7 %copy-done.4 = f32[512]{0:T(512)S(1)} copy-done((f32[512]{0:T(512)S(1)}, f32[512]{0:T(512)}, u32[]{:S(2)}) %copy-start.4) | copy-done | bytes 2072
  5.7 0.0 copy-start.5
  5.7 0.7 %copy-done.5 = f32[512]{0:T(512)S(1)} copy-done((f32[512]{0:T(512)S(1)}, f32[512]{0:T(512)}, u32[]{:S(2)}) %copy-start.5) | copy-done | bytes 2072
  6.4 0.0 copy-start.6
  6.4 0.7 %copy-done.6 = f32[512]{0:T(512)S(1)} copy-done((f32[512]{0:T(512)S(1)}, f32[512]{0:T(512)}, u32[]{:S(2)}) %copy-start.6) | copy-done | bytes 2072
  7.0 46.1 %swin_window_attention.1 = bf16[2,12,48,512]{3,2,1,0:T(8,128)(2,1)S(1)} custom-call(bf16[2,12,48,512]{3,2,1,0:T(8,128)(2,1)S(1)} %copy-done.1, bf16[512,1536]{1,0:T(8,128)(2,1)S(1)} %copy-done, bf16[512,512]{1,0:T(8,128)(2,1)S(1)} %copy-done.3, f32[1,512]{1,0:T(1,128)S(1)} %bitcast.3, f32[1,512]{1,0:T(1,128)S(1)} %bitcast.4, f32[1,512]{1,0:T(1,128)S(1)} %bitcast.5, ...), custom_call_target="tpu_custom_call" | custom-call | tf_op jit(solution)/shard_map/swin_window_attention/pallas_call | solution.py:275
  53.1 1.0 %copy.9 = bf16[2,12,48,512]{3,2,1,0:T(8,128)(2,1)} copy(bf16[2,12,48,512]{3,2,1,0:T(8,128)(2,1)S(1)} %swin_window_attention.1) | data formatting | bytes 2359296
Async XLA Ops:
  0.0 1.4 %copy-start = (bf16[512,1536]{1,0:T(8,128)(2,1)S(1)}, bf16[512,1536]{1,0:T(8,128)(2,1)}, u32[]{:S(2)}) copy-start(bf16[512,1536]{1,0:T(8,128)(2,1)} %wqkv_h.1) | copy-start | bytes 4718596
  1.4 1.3 %copy-start.1 = (bf16[2,12,48,512]{3,2,1,0:T(8,128)(2,1)S(1)}, bf16[2,12,48,512]{3,2,1,0:T(8,128)(2,1)}, u32[]{:S(2)}) copy-start(bf16[2,12,48,512]{3,2,1,0:T(8,128)(2,1)} %lat_h.1) | copy-start | bytes 3538948
  2.7 1.3 %copy-start.2 = (bf16[2,8,144,144]{3,2,1,0:T(8,128)(2,1)S(1)}, bf16[2,8,144,144]{3,2,1,0:T(8,128)(2,1)}, u32[]{:S(2)}) copy-start(bf16[2,8,144,144]{3,2,1,0:T(8,128)(2,1)} %bias_h.1) | copy-start | bytes 1990660
  4.0 1.0 %copy-start.3 = (bf16[512,512]{1,0:T(8,128)(2,1)S(1)}, bf16[512,512]{1,0:T(8,128)(2,1)}, u32[]{:S(2)}) copy-start(bf16[512,512]{1,0:T(8,128)(2,1)} %wout_h.1) | copy-start | bytes 1572868
  5.0 0.7 %copy-start.4 = (f32[512]{0:T(512)S(1)}, f32[512]{0:T(512)}, u32[]{:S(2)}) copy-start(f32[512]{0:T(512)} %param.10) | copy-start | bytes 6148
  5.7 0.7 %copy-start.5 = (f32[512]{0:T(512)S(1)}, f32[512]{0:T(512)}, u32[]{:S(2)}) copy-start(f32[512]{0:T(512)} %param.11) | copy-start | bytes 6148
  6.4 0.7 %copy-start.6 = (f32[512]{0:T(512)S(1)}, f32[512]{0:T(512)}, u32[]{:S(2)}) copy-start(f32[512]{0:T(512)} %param.12) | copy-start | bytes 6148

commit v2 on v0

v2 whole, which is shorter than its diff:
```python
import functools

import jax
import jax.numpy as jnp
from jax import lax
from jax.experimental import pallas as pl
from jax.experimental.pallas import tpu as pltpu
from jax.sharding import PartitionSpec as P

LEV = 2
WLAT = 6
WLON = 12
SLAT = 3
SLON = 6
WT = 144
HEADS = 8
D = 512
LT = 4
GROUP = 4
F32 = jnp.float32
BF16 = jnp.bfloat16
MESH = pl.DeviceIdType.MESH

(C_N, C_M, C_S, C_WQKV, C_WOUT, C_BIAS, C_B, C_G, C_H) = range(9)
XA, XB, XR, XF, RA, RB, RR, RF = range(0, 32, 4)
EM, ES, COR, WM, WS, DIAG = range(32, 38)
COPIES = 38

X_CUTS = ((0, 48, 80), (80, 128, 160), (160, 192, 224), (224, 256, 288))
X_CORNER_E = 36
X_WINDOW = 72
R_CUTS = ((0, 16, 32), (32, 64, 96), (96, 144, 176), (176, 224, 256))
R_WINDOW = 36


def kernel(
    nlat, nlon,
    lat_h, wqkv_h, wout_h, b_h, gain_h, shift_h, bias_h, out_v,
    lat_v, wqkv, wout, b_out, gain, shift, bias_v, biasf, fx, pf, win_in, win_out,
    stage, stage_r, xs, xr, xrelay, rs, rr, rrelay, cmp_f, s80, s48, r80, r48, cor,
    lsem, ssem, rsem,
):
    ilat, ilon = lax.axis_index("lat"), lax.axis_index("lon")

    def at(dlat, dlon):
        return {
            "lat": lax.rem(ilat + dlat + nlat, nlat),
            "lon": lax.rem(ilon + dlon + nlon, nlon),
        }

    place = lax.rem(ilat, GROUP)
    head, tail = place == 0, place == GROUP - 1
    inner = jnp.logical_and(place != 0, place != GROUP - 1)

    barrier = pltpu.get_barrier_semaphore()

    def greet(who):
        pl.semaphore_signal(barrier, inc=1, device_id=who, device_id_type=MESH)

    for who in (at(-1, 0), at(1, 0), at(0, -1), at(0, 1), at(-1, -1), at(1, 1)):
        greet(who)

    @pl.when(head)
    def _():
        for who in (at(GROUP - 1, 0), at(GROUP, 0), at(-GROUP, 0)):
            greet(who)

    @pl.when(tail)
    def _():
        for who in (at(1 - GROUP, 0), at(GROUP, 0), at(-GROUP, 0)):
            greet(who)

    def local(src, dst, which):
        return pltpu.make_async_copy(src, dst, lsem.at[which])

    def remote(src, dst, which, who, send=None):
        return pltpu.make_async_remote_copy(
            src_ref=src, dst_ref=dst, send_sem=ssem.at[which if send is None else send],
            recv_sem=rsem.at[which], device_id=who, device_id_type=MESH,
        )

    loads = {
        C_N: local(lat_h.at[:, 0:3], lat_v.at[:, 0:3], C_N),
        C_M: local(lat_h.at[:, 3:9], lat_v.at[:, 3:9], C_M),
        C_S: local(lat_h.at[:, 9:12], lat_v.at[:, 9:12], C_S),
        C_BIAS: local(bias_h, bias_v, C_BIAS),
        C_WQKV: local(wqkv_h, wqkv, C_WQKV),
        C_WOUT: local(wout_h, wout, C_WOUT),
        C_B: local(b_h, b_out, C_B),
        C_G: local(gain_h, gain, C_G),
        C_H: local(shift_h, shift, C_H),
    }
    for copy in loads.values():
        copy.start()

    def rows(ref, a, b):
        return ref.at[a:b]

    def x_direct(k):
        a, m, _ = X_CUTS[k]
        return remote(rows(xs, a, m), rows(xr, a, m), XA + k, at(-1, 0))

    def x_other(k):
        _, m, b = X_CUTS[k]
        return remote(rows(xs, m, b), rows(xr, m, b), XB + k, at(-1, 0))

    def x_around(k):
        _, m, b = X_CUTS[k]
        return remote(rows(xs, m, b), rows(xrelay, m, b), XR + k, at(GROUP - 1, 0), XB + k)

    def x_forward(k):
        _, m, b = X_CUTS[k]
        return remote(rows(xrelay, m, b), rows(xr, m, b), XB + k, at(-GROUP, 0), XF + k)

    def r_direct(k):
        a, m, _ = R_CUTS[k]
        return remote(rows(rs, a, m), rows(rr, a, m), RA + k, at(1, 0))

    def r_other(k):
        _, m, b = R_CUTS[k]
        return remote(rows(rs, m, b), rows(rr, m, b), RB + k, at(1, 0))

    def r_around(k):
        _, m, b = R_CUTS[k]
        return remote(rows(rs, m, b), rows(rrelay, m, b), RR + k, at(1 - GROUP, 0), RB + k)

    def r_forward(k):
        _, m, b = R_CUTS[k]
        return remote(rows(rrelay, m, b), rows(rr, m, b), RB + k, at(GROUP, 0), RF + k)

    def x_send(k):
        pl.when(head)(x_around(k).start)
        pl.when(jnp.logical_not(head))(x_other(k).start)
        x_direct(k).start()

    def r_send(k):
        pl.when(tail)(r_around(k).start)
        pl.when(jnp.logical_not(tail))(r_other(k).start)
        r_direct(k).start()

    def x_relay(k):
        @pl.when(tail)
        def _():
            x_around(k).wait_recv()
            x_forward(k).start()

    def r_relay(k):
        @pl.when(head)
        def _():
            r_around(k).wait_recv()
            r_forward(k).start()

    em = remote(s80.at[0], r80.at[0], EM, at(0, -1))
    es = remote(s48.at[0], r48.at[0], ES, at(0, -1))
    corner = remote(rows(xr, 0, 48), cor, COR, at(0, -1))
    wm = remote(s80.at[1], r80.at[1], WM, at(0, 1))
    ws = remote(s48.at[1], r48.at[1], WS, at(0, 1))
    diag = remote(s48.at[2], r48.at[2], DIAG, at(1, 1))

    def widen(src, dst, a, b):
        for t in range(LT):
            dst[t, a:b, :] = src[a:b, 128 * t : 128 * (t + 1)].astype(F32)

    def narrow(src, dst, a, b):
        for t in range(LT):
            dst[a:b, 128 * t : 128 * (t + 1)] = src[t, a:b, :].astype(BF16)

    def spread(row0, row1):
        for l in range(LEV):
            for row in range(row0, row1):
                for t in range(LT):
                    fx[t, l, row, 0:48] = lat_v[l, row, :, 128 * t : 128 * (t + 1)].astype(F32)

    loads[C_N].wait()
    spread(0, 3)
    n = 0
    for col, width in ((0, 6), (42, 6), (6, 12), (18, 12), (30, 12)):
        for l in range(LEV):
            for i in range(SLAT):
                stage[:, n : n + width, :] = fx[:, l, i, col : col + width, :]
                n += width
    narrow(stage, xs, 0, 288)

    loads[C_M].wait()
    spread(3, 9)
    n = 0
    for l in range(LEV):
        for row in range(3, 9):
            cmp_f[0, :, n : n + SLON, :] = fx[:, l, row, 0:SLON, :]
            n += SLON
    narrow(cmp_f.at[0], s80.at[0], 0, 80)
    loads[C_S].wait()
    spread(9, 12)
    n = 0
    for l in range(LEV):
        for row in range(9, 12):
            cmp_f[1, :, n : n + SLON, :] = fx[:, l, row, 0:SLON, :]
            n += SLON
    narrow(cmp_f.at[1], s48.at[0], 0, 48)

    loads[C_BIAS].wait()
    is_last = ilat == nlat - 1

    def south_half(axis):
        n = lax.broadcasted_iota(jnp.int32, (WT, WT), axis)
        return jnp.logical_or(jnp.logical_and(n >= 36, n < 72), n >= 108)

    apart = jnp.logical_and(south_half(0) != south_half(1), is_last)
    penalty = jnp.where(apart, F32(-1e30), F32(0.0))
    for r in range(2):
        for h in range(HEADS):
            value = bias_v[r, h].astype(F32)
            biasf[r, h // 2, WT * (h % 2) : WT * (h % 2 + 1), :] = value + penalty if r else value

    lane = lax.broadcasted_iota(jnp.int32, (1, 128), 1)
    first = lane < 64
    scale0 = jnp.where(first, F32(0.125), F32(0.0))
    scale1 = jnp.where(first, F32(0.0), F32(0.125))

    def attend(r, x):
        qkv = jnp.dot(x, wqkv[...], preferred_element_type=F32)
        parts = []
        for p in range(HEADS // 2):
            qf = qkv[:, 128 * p : 128 * (p + 1)]
            kp = qkv[:, D + 128 * p : D + 128 * (p + 1)].astype(BF16)
            vp = qkv[:, 2 * D + 128 * p : 2 * D + 128 * (p + 1)].astype(BF16)
            q2 = jnp.concatenate([(qf * scale0).astype(BF16), (qf * scale1).astype(BF16)], 0)
            s = lax.dot_general(q2, kp, (((1,), (1,)), ((), ())), preferred_element_type=F32)
            s = s + biasf[r, p]
            e = jnp.exp(s - jnp.max(s, axis=-1, keepdims=True)).astype(BF16)
            vx = jnp.concatenate([vp, jnp.ones((WT, 128), BF16)], 1)
            o = jnp.dot(e, vx, preferred_element_type=F32)
            num = jnp.where(first, o[:WT, :128], o[WT:, :128])
            den = jnp.where(first, o[:WT, 128:], o[WT:, 128:])
            parts.append((num / den).astype(BF16))
        att = jnp.concatenate(parts, 1)
        proj = jnp.dot(att, wout[...], preferred_element_type=F32) + b_out[...]
        return proj.astype(BF16).astype(F32)

    def token(l, i):
        return WLON * (WLAT * l + i)

    def compute(r, slot):
        x = jnp.concatenate([win_in[slot, t].astype(BF16) for t in range(LT)], 1)
        proj = attend(r, x)
        for t in range(LT):
            win_out[slot, t] = proj[:, 128 * t : 128 * (t + 1)]

    def take(slot, i0, i1, row0, col):
        for l in range(LEV):
            for i in range(i0, i1):
                j = token(l, i)
                win_in[slot, :, j : j + WLON, :] = fx[:, l, row0 + i - i0, col : col + WLON, :]

    def keep(slot, i1, row0, col, own):
        for l in range(LEV):
            for i in range(i1):
                j = token(l, i)
                pf[:, l, row0 + i, col : col + own, :] = win_out[slot, :, j : j + own, :]

    def pack(slot, i0, i1, off, width, dst, n):
        for l in range(LEV):
            for i in range(i0, i1):
                j = token(l, i) + off
                dst[:, n : n + width, :] = win_out[slot, :, j : j + width, :]
                n += width

    def window_m(b):
        slot = b % 2
        col = SLON + WLON * b
        take(slot, 0, WLAT, 3, col)
        compute(0, slot)
        keep(slot, WLAT, 3, col, WLON if b < 3 else SLON)
        if b == 3:
            pack(slot, 0, WLAT, SLON, SLON, cmp_f.at[0], 0)
            narrow(cmp_f.at[0], s80.at[1], 0, 80)
            wm.start()

    def window_s(b):
        slot = b % 2
        col = SLON + WLON * b
        take(slot, 0, SLAT, 9, col)
        for l in range(LEV):
            j = token(l, SLAT)
            if b < 3:
                n = X_WINDOW + 72 * b + 36 * l
                win_in[slot, :, j : j + 36, :] = stage[:, n : n + 36, :]
            else:
                for i in range(SLAT):
                    n = SLON * (SLAT * l + i)
                    jj = j + WLON * i
                    win_in[slot, :, jj : jj + SLON, :] = stage[
                        :, X_CORNER_E + n : X_CORNER_E + n + SLON, :
                    ]
                    win_in[slot, :, jj + SLON : jj + WLON, :] = cmp_f[1, :, n : n + SLON, :]
        compute(1, slot)
        if b == 3:
            pack(slot, SLAT, WLAT, 0, SLON, stage_r, 0)
            narrow(stage_r, rs, *R_CUTS[0][::2])
            r_send(0)
            pack(slot, SLAT, WLAT, SLON, SLON, cmp_f.at[0], 0)
            narrow(cmp_f.at[0], s48.at[2], 0, 48)
            diag.start()
            pack(slot, 0, SLAT, SLON, SLON, cmp_f.at[1], 0)
            narrow(cmp_f.at[1], s48.at[1], 0, 48)
            ws.start()
        else:
            for l in range(LEV):
                n, j = R_WINDOW + 72 * b + 36 * l, token(l, SLAT)
                stage_r[:, n : n + 36, :] = win_out[slot, :, j : j + 36, :]
            narrow(stage_r, rs, *R_CUTS[b + 1][::2])
            r_send(b + 1)
        keep(slot, SLAT, 9, col, WLON if b < 3 else SLON)

    loads[C_WQKV].wait()
    loads[C_WOUT].wait()
    loads[C_B].wait()
    for b in range(3):
        window_m(b)

    pl.when(inner)(lambda: pl.semaphore_wait(barrier, 6))
    pl.when(jnp.logical_not(inner))(lambda: pl.semaphore_wait(barrier, 9))
    for k in range(4):
        x_send(k)
    em.start()
    es.start()
    x_relay(0)
    x_relay(1)
    em.wait_recv()
    widen(r80.at[0], cmp_f.at[0], 0, 80)
    n = 0
    for l in range(LEV):
        for row in range(3, 9):
            fx[:, l, row, 48 : 48 + SLON, :] = cmp_f[0, :, n : n + SLON, :]
            n += SLON
    window_m(3)
    x_relay(2)
    x_relay(3)

    def x_take(k):
        x_direct(k).wait_recv()
        x_other(k).wait_recv()
        if k == 0:
            corner.start()
        widen(xr, stage, *X_CUTS[k][::2])

    x_take(0)
    es.wait_recv()
    widen(r48.at[0], cmp_f.at[0], 0, 48)
    n = 0
    for l in range(LEV):
        for row in range(9, 12):
            fx[:, l, row, 48 : 48 + SLON, :] = cmp_f[0, :, n : n + SLON, :]
            n += SLON
    corner.wait_recv()
    widen(cor, cmp_f.at[1], 0, 48)
    window_s(3)
    for b in range(3):
        x_take(b + 1)
        window_s(b)
    r_relay(0)

    loads[C_G].wait()
    loads[C_H].wait()

    def finish(row0, row1):
        for l in range(LEV):
            for row in range(row0, row1):
                v = jnp.concatenate([pf[t, l, row] for t in range(LT)], 1)
                mean = jnp.mean(v, axis=-1, keepdims=True)
                d = v - mean
                var = jnp.mean(d * d, axis=-1, keepdims=True)
                normed = d * lax.rsqrt(var + F32(1e-5)) * gain[...] + shift[...]
                out_v[l, row] = (lat_v[l, row].astype(F32) + normed).astype(BF16)

    def place_rows(src, n, width, row0, count, col):
        for l in range(LEV):
            for i in range(count):
                pf[:, l, row0 + i, col : col + width, :] = src[:, n : n + width, :]
                n += width

    wm.wait_recv()
    widen(r80.at[1], cmp_f.at[0], 0, 80)
    place_rows(cmp_f.at[0], 0, SLON, 3, WLAT, 0)
    finish(3, 9)
    r_relay(1)
    ws.wait_recv()
    widen(r48.at[1], cmp_f.at[1], 0, 48)
    place_rows(cmp_f.at[1], 0, SLON, 9, SLAT, 0)
    finish(9, 12)
    r_relay(2)
    r_relay(3)
    diag.wait_recv()
    widen(r48.at[2], cmp_f.at[1], 0, 48)
    place_rows(cmp_f.at[1], 0, SLON, 0, SLAT, 0)
    groups = [(36 * l + WLON * i + 72 * b + R_WINDOW, WLON, l, i, SLON + WLON * b)
              for b in range(3) for l in range(LEV) for i in range(SLAT)]
    groups += [(SLON * (SLAT * l + i), SLON, l, i, 42) for l in range(LEV) for i in range(SLAT)]
    for k in range(4):
        r_direct(k).wait_recv()
        r_other(k).wait_recv()
        a, _, b = R_CUTS[k]
        widen(rr, stage, a, b)
        for n, width, l, i, col in groups:
            if a < n + width <= b:
                pf[:, l, i, col : col + width, :] = stage[:, n : n + width, :]
    finish(0, 3)

    for copy in (em, es, corner, wm, ws, diag):
        copy.wait_send()
    for k in range(4):
        x_direct(k).wait_send()
        x_other(k).wait_send()
        r_direct(k).wait_send()
        r_other(k).wait_send()
        pl.when(tail)(x_forward(k).wait_send)
        pl.when(head)(r_forward(k).wait_send)


def local_step(nlat, nlon, latent, w_qkv, w_out, b_out, norm_gain, norm_shift, earth_bias):
    hbm = pl.BlockSpec(memory_space=pl.ANY)
    tile = latent.shape
    return pl.pallas_call(
        functools.partial(kernel, nlat, nlon),
        out_shape=pltpu.VMEM(tile, BF16),
        in_specs=[hbm] * 7,
        out_specs=pl.BlockSpec(memory_space=pltpu.VMEM),
        scratch_shapes=[
            pltpu.VMEM(tile, BF16),
            pltpu.VMEM((D, 3 * D), BF16),
            pltpu.VMEM((D, D), BF16),
            pltpu.VMEM((1, D), F32),
            pltpu.VMEM((1, D), F32),
            pltpu.VMEM((1, D), F32),
            pltpu.VMEM((2, HEADS, WT, WT), BF16),
            pltpu.VMEM((2, HEADS // 2, 2 * WT, WT), F32),
            pltpu.VMEM((LT, LEV, 12, 64, 128), F32),
            pltpu.VMEM((LT, LEV, 12, 48, 128), F32),
            pltpu.VMEM((2, LT, WT, 128), F32),
            pltpu.VMEM((2, LT, WT, 128), F32),
            pltpu.VMEM((LT, 288, 128), F32),
            pltpu.VMEM((LT, 256, 128), F32),
            pltpu.VMEM((288, D), BF16),
            pltpu.VMEM((288, D), BF16),
            pltpu.VMEM((288, D), BF16),
            pltpu.VMEM((256, D), BF16),
            pltpu.VMEM((256, D), BF16),
            pltpu.VMEM((256, D), BF16),
            pltpu.VMEM((2, LT, 80, 128), F32),
            pltpu.VMEM((2, 80, D), BF16),
            pltpu.VMEM((3, 48, D), BF16),
            pltpu.VMEM((2, 80, D), BF16),
            pltpu.VMEM((3, 48, D), BF16),
            pltpu.VMEM((48, D), BF16),
            pltpu.SemaphoreType.DMA((9,)),
            pltpu.SemaphoreType.DMA((COPIES,)),
            pltpu.SemaphoreType.DMA((COPIES,)),
        ],
        compiler_params=pltpu.CompilerParams(
            collective_id=0, has_side_effects=True, vmem_limit_bytes=60 * 1024 * 1024
        ),
        name="swin_window_attention",
    )(
        latent, w_qkv, w_out, b_out.reshape(1, D), norm_gain.reshape(1, D),
        norm_shift.reshape(1, D), earth_bias,
    )


def solution(mesh):
    placed = (P(None, "lat", "lon", None), P(), P(), P(), P(), P(), P("lat", None, None, None))
    step = functools.partial(local_step, mesh.shape["lat"], mesh.shape["lon"])
    return jax.shard_map(
        step, mesh=mesh, in_specs=placed, out_specs=P(None, "lat", "lon", None), check_vma=False
    )
```

time: 126 us -> 41.4 us (0.33); the launches traced: 124 us -> 41.2 us
  local copies, waits for them, and re-layouts: 47.4 us -> 1.02 us
  Pallas kernels: 0 us -> 40.2 us
  waiting for transfers between devices: 29.2 us -> 0 us
  starting transfers between devices: 24.6 us -> 0 us
  matrix products: 14.5 us -> 0 us
  other arithmetic: 8 us -> 0 us
    pallas_call x0 -> x1, Pallas kernels: none -> 40.2 us  [local_step(): pl.pallas_call(functools.partial(kernel, nlat, nlon), out_shape=pltpu.VME...]
    ppermute x4 -> x0, waiting for transfers between devices: 29.2 us -> none  [shifted(): lax.ppermute(shard, axis, [(i, (i + by) % size) for i in range(size)])]
    ppermute x4 -> x0, starting transfers between devices: 24.6 us -> none  [shifted(): lax.ppermute(shard, axis, [(i, (i + by) % size) for i in range(size)])]
    dot_general x4 -> x0, matrix products: 14.5 us -> none  [the longest x1 6.04 us: local(): jnp.einsum('abhqk,abkhe->abqhe', probs, values, preferred_element_type=jn...]
    unnamed x23 -> x1, local copies, waits for them, and re-layouts: 13.6 us -> 1.02 us
    slice x6 -> x0, local copies, waits for them, and re-layouts: 9.93 us -> none  [the longest x1 6.14 us: local(): query, keys, values = (wins[:, :, :, 0], wins[:, :, :, 1], wins[:, :, :, 2])]
    reshape x1 -> x0, local copies, waits for them, and re-layouts: 9.53 us -> none  [local(): wins = qkv.reshape(nwl, nwo, WT, 3, heads, head_dim)]
    convert_element_type x2 -> x0, local copies, waits for them, and re-layouts: 7.58 us -> none  [the longest x1 4.75 us: local(): attended = attended.astype(jnp.bfloat16).reshape(nwl, nwo, WT, width)]
  transfers between devices with their start and end apart: 4 -> 0, of which waited for: 3 -> 0; matrix products, arithmetic and copies ran while one was open for 5% -> 0% of each run, Pallas kernels for 0% -> 0%
where the time goes in v2:
time: 41.4 us; the launch traced here: 41.2 us
  Pallas kernels  40.2 us (97%)
  local copies, waits for them, and re-layouts  1.02 us (2%)
    pallas_call x1, Pallas kernels, local_step(): pl.pallas_call(functools.partial(kernel, nlat, nlon), out_shape=pltpu.VME...  40.2 us
    unnamed x1, local copies, waits for them, and re-layouts  1.02 us

profile of v2, /device:TPU:1, one launch (start us, length us, event | category | flops | bytes accessed | tf_op | source)
XLA Modules:
  0.0 41.2 jit_solution(14327503926162347269)
XLA Ops:
  0.0 40.2 %swin_window_attention.1 = bf16[2,12,48,512]{3,2,1,0:T(8,128)(2,1)S(1)} custom-call(bf16[2,12,48,512]{3,2,1,0:T(8,128)(2,1)} %lat_h.1, bf16[512,1536]{1,0:T(8,128)(2,1)} %wqkv_h.1, bf16[512,512]{1,0:T(8,128)(2,1)} %wout_h.1, f32[1,512]{1,0:T(1,128)} %bitcast.3, f32[1,512]{1,0:T(1,128)} %bitcast.4, f32[1,512]{1,0:T(1,128)} %bitcast.5, ...), custom_call_target="tpu_custom_call" | custom-call | tf_op jit(solution)/shard_map/swin_window_attention/pallas_call | solution.py:423
  40.2 1.0 %copy.9 = bf16[2,12,48,512]{3,2,1,0:T(8,128)(2,1)} copy(bf16[2,12,48,512]{3,2,1,0:T(8,128)(2,1)S(1)} %swin_window_attention.1) | data formatting | bytes 2359296

commit v3 on v2

--- a/solution.py
+++ b/solution.py
@@ -23,21 +23,25 @@
 
 (C_N, C_M, C_S, C_WQKV, C_WOUT, C_BIAS, C_B, C_G, C_H) = range(9)
 XA, XB, XR, XF, RA, RB, RR, RF = range(0, 32, 4)
-EM, ES, COR, WM, WS, DIAG = range(32, 38)
-COPIES = 38
+BA, BP, EM, ES, EN, COR, CORN, WM, WS, WN, DIAG = range(32, 43)
+COPIES = 43
 
 X_CUTS = ((0, 48, 80), (80, 128, 160), (160, 192, 224), (224, 256, 288))
+T_CUTS = ((0, 32, 80), (80, 112, 160), (160, 176, 224), (224, 240, 288))
 X_CORNER_E = 36
 X_WINDOW = 72
-R_CUTS = ((0, 16, 32), (32, 64, 96), (96, 144, 176), (176, 224, 256))
-R_WINDOW = 36
+R_CUTS = ((0, 64), (64, 144), (144, 208), (208, 256))
+R_CORNER = 216
+B_ROWS = 336
+HALF = WT // 2
 
 
 def kernel(
     nlat, nlon,
     lat_h, wqkv_h, wout_h, b_h, gain_h, shift_h, bias_h, out_v,
     lat_v, wqkv, wout, b_out, gain, shift, bias_v, biasf, fx, pf, win_in, win_out,
-    stage, stage_r, xs, xr, xrelay, rs, rr, rrelay, cmp_f, s80, s48, r80, r48, cor,
+    stage, stage_n, stage_r, xs, xr, xrelay, rs, rr, rrelay, bt, bstage, bs, br, bp,
+    cmp_f, s80, s48, r80, r48, cor, corn,
     lsem, ssem, rsem,
 ):
     ilat, ilon = lax.axis_index("lat"), lax.axis_index("lon")
@@ -48,9 +52,15 @@
             "lon": lax.rem(ilon + dlon + nlon, nlon),
         }
 
+    core = lax.rem(ilon, 2)
     place = lax.rem(ilat, GROUP)
     head, tail = place == 0, place == GROUP - 1
     inner = jnp.logical_and(place != 0, place != GROUP - 1)
+    not_head, not_tail = jnp.logical_not(head), jnp.logical_not(tail)
+    late_send = ilat == 0
+    early_send = jnp.logical_not(late_send)
+    forward_first = jnp.logical_and(head, early_send)
+    forward_last = late_send
 
     barrier = pltpu.get_barrier_semaphore()
 
@@ -80,10 +90,10 @@
         )
 
     loads = {
+        C_S: local(lat_h.at[:, 9:12], lat_v.at[:, 9:12], C_S),
         C_N: local(lat_h.at[:, 0:3], lat_v.at[:, 0:3], C_N),
+        C_BIAS: local(bias_h, bias_v, C_BIAS),
         C_M: local(lat_h.at[:, 3:9], lat_v.at[:, 3:9], C_M),
-        C_S: local(lat_h.at[:, 9:12], lat_v.at[:, 9:12], C_S),
-        C_BIAS: local(bias_h, bias_v, C_BIAS),
         C_WQKV: local(wqkv_h, wqkv, C_WQKV),
         C_WOUT: local(wout_h, wout, C_WOUT),
         C_B: local(b_h, b_out, C_B),
@@ -112,31 +122,32 @@
         _, m, b = X_CUTS[k]
         return remote(rows(xrelay, m, b), rows(xr, m, b), XB + k, at(-GROUP, 0), XF + k)
 
-    def r_direct(k):
-        a, m, _ = R_CUTS[k]
+    def t_direct(k):
+        a, m, _ = T_CUTS[k]
         return remote(rows(rs, a, m), rows(rr, a, m), RA + k, at(1, 0))
 
-    def r_other(k):
-        _, m, b = R_CUTS[k]
-        return remote(rows(rs, m, b), rows(rr, m, b), RB + k, at(1, 0))
-
-    def r_around(k):
-        _, m, b = R_CUTS[k]
+    def t_around(k):
+        _, m, b = T_CUTS[k]
         return remote(rows(rs, m, b), rows(rrelay, m, b), RR + k, at(1 - GROUP, 0), RB + k)
 
-    def r_forward(k):
-        _, m, b = R_CUTS[k]
+    def t_forward(k):
+        _, m, b = T_CUTS[k]
         return remote(rows(rrelay, m, b), rows(rr, m, b), RB + k, at(GROUP, 0), RF + k)
+
+    b_direct = remote(bs, br, BA, at(1, 0))
+    b_pair = remote(br, bp, BP, at(0, 1 - 2 * core))
+
+    def r_copy(k):
+        return remote(rows(rs, *R_CUTS[k]), rows(rr, *R_CUTS[k]), RA + k, at(1, 0))
 
     def x_send(k):
         pl.when(head)(x_around(k).start)
-        pl.when(jnp.logical_not(head))(x_other(k).start)
+        pl.when(not_head)(x_other(k).start)
         x_direct(k).start()
 
-    def r_send(k):
-        pl.when(tail)(r_around(k).start)
-        pl.when(jnp.logical_not(tail))(r_other(k).start)
-        r_direct(k).start()
+    def t_send(k):
+        t_around(k).start()
+        t_direct(k).start()
 
     def x_relay(k):
         @pl.when(tail)
@@ -144,17 +155,20 @@
             x_around(k).wait_recv()
             x_forward(k).start()
 
-    def r_relay(k):
-        @pl.when(head)
+    def t_relay(k, when):
+        @pl.when(when)
         def _():
-            r_around(k).wait_recv()
-            r_forward(k).start()
+            t_around(k).wait_recv()
+            t_forward(k).start()
 
     em = remote(s80.at[0], r80.at[0], EM, at(0, -1))
     es = remote(s48.at[0], r48.at[0], ES, at(0, -1))
+    en = remote(s48.at[3], r48.at[3], EN, at(0, -1))
     corner = remote(rows(xr, 0, 48), cor, COR, at(0, -1))
+    corner_n = remote(rows(rr, 0, 48), corn, CORN, at(0, -1))
     wm = remote(s80.at[1], r80.at[1], WM, at(0, 1))
     ws = remote(s48.at[1], r48.at[1], WS, at(0, 1))
+    wn = remote(s48.at[4], r48.at[4], WN, at(0, 1))
     diag = remote(s48.at[2], r48.at[2], DIAG, at(1, 1))
 
     def widen(src, dst, a, b):
@@ -171,34 +185,78 @@
                 for t in range(LT):
                     fx[t, l, row, 0:48] = lat_v[l, row, :, 128 * t : 128 * (t + 1)].astype(F32)
 
+    def pack_stream(dst_f, dst, row0):
+        n = 0
+        for col, width in ((0, 6), (42, 6), (6, 12), (18, 12), (30, 12)):
+            for l in range(LEV):
+                for i in range(SLAT):
+                    dst_f[:, n : n + width, :] = fx[:, l, row0 + i, col : col + width, :]
+                    n += width
+        narrow(dst_f, dst, 0, 288)
+
+    def pack_west(slot, dst, row0, row1, size):
+        n = 0
+        for l in range(LEV):
+            for row in range(row0, row1):
+                cmp_f[slot, :, n : n + SLON, :] = fx[:, l, row, 0:SLON, :]
+                n += SLON
+        narrow(cmp_f.at[slot], dst, 0, size)
+
+    def unpack_east(src, slot, row0, row1, size):
+        widen(src, cmp_f.at[slot], 0, size)
+        n = 0
+        for l in range(LEV):
+            for row in range(row0, row1):
+                fx[:, l, row, 48 : 48 + SLON, :] = cmp_f[slot, :, n : n + SLON, :]
+                n += SLON
+
+    loads[C_S].wait()
+    spread(9, 12)
+
+    @pl.when(tail)
+    def _():
+        pack_stream(stage_n, rs, 9)
+        pl.semaphore_wait(barrier, 9)
+        t_send(0)
+
+    pack_west(1, s48.at[0], 9, 12, 48)
+    loads[C_BIAS].wait()
+
+    @pl.when(tail)
+    def _():
+        bt[HEADS] = jnp.concatenate(
+            [bias_v[1, h].astype(F32)[:, 128:WT] for h in range(HEADS)], 1
+        )
+        for g in range(4):
+            bt[g] = bias_v[1, 4 * core + g, :, 0:128].astype(F32)
+            bstage[HALF * g : HALF * g + 36, :] = bt[g, 36:72, :]
+            bstage[HALF * g + 36 : HALF * (g + 1), :] = bt[g, 108:WT, :]
+        for c in range(2):
+            @pl.when(core == c)
+            def _():
+                bstage[4 * HALF : 4 * HALF + 36, :] = bt[HEADS, 36 + 72 * c : 72 + 72 * c, :]
+        bs[...] = bstage[...].astype(BF16)
+        b_direct.start()
+
     loads[C_N].wait()
     spread(0, 3)
-    n = 0
-    for col, width in ((0, 6), (42, 6), (6, 12), (18, 12), (30, 12)):
-        for l in range(LEV):
-            for i in range(SLAT):
-                stage[:, n : n + width, :] = fx[:, l, i, col : col + width, :]
-                n += width
-    narrow(stage, xs, 0, 288)
-
+    pack_stream(stage, xs, 0)
     loads[C_M].wait()
     spread(3, 9)
-    n = 0
-    for l in range(LEV):
-        for row in range(3, 9):
-            cmp_f[0, :, n : n + SLON, :] = fx[:, l, row, 0:SLON, :]
-            n += SLON
-    narrow(cmp_f.at[0], s80.at[0], 0, 80)
-    loads[C_S].wait()
-    spread(9, 12)
-    n = 0
-    for l in range(LEV):
-        for row in range(9, 12):
-            cmp_f[1, :, n : n + SLON, :] = fx[:, l, row, 0:SLON, :]
-            n += SLON
-    narrow(cmp_f.at[1], s48.at[0], 0, 48)
-
-    loads[C_BIAS].wait()
+    pack_west(0, s80.at[0], 3, 9, 80)
+    pl.when(head)(lambda: pack_west(1, s48.at[3], 0, 3, 48))
+
+    def greet_and_send():
+        pl.when(inner)(lambda: pl.semaphore_wait(barrier, 6))
+        pl.when(head)(lambda: pl.semaphore_wait(barrier, 9))
+        x_send(0)
+        em.start()
+        es.start()
+        pl.when(head)(en.start)
+        x_send(1)
+
+    pl.when(early_send)(greet_and_send)
+
     is_last = ilat == nlat - 1
 
     def south_half(axis):
@@ -294,71 +352,120 @@
                     ]
                     win_in[slot, :, jj + SLON : jj + WLON, :] = cmp_f[1, :, n : n + SLON, :]
         compute(1, slot)
+
+        @pl.when(not_tail)
+        def _():
+            if b == 3:
+                pack(slot, SLAT, WLAT, 0, SLON, stage_r, R_CORNER)
+            else:
+                for l in range(LEV):
+                    n, j = 72 * b + 36 * l, token(l, SLAT)
+                    stage_r[:, n : n + 36, :] = win_out[slot, :, j : j + 36, :]
+            narrow(stage_r, rs, *R_CUTS[b])
+            if b == 3:
+                r_copy(b).start()
+                pack(slot, SLAT, WLAT, SLON, SLON, cmp_f.at[0], 0)
+                narrow(cmp_f.at[0], s48.at[2], 0, 48)
+                diag.start()
+            elif b == 2:
+                r_copy(b).start()
+            else:
+                pl.when(early_send)(r_copy(b).start)
+
         if b == 3:
-            pack(slot, SLAT, WLAT, 0, SLON, stage_r, 0)
-            narrow(stage_r, rs, *R_CUTS[0][::2])
-            r_send(0)
-            pack(slot, SLAT, WLAT, SLON, SLON, cmp_f.at[0], 0)
-            narrow(cmp_f.at[0], s48.at[2], 0, 48)
-            diag.start()
             pack(slot, 0, SLAT, SLON, SLON, cmp_f.at[1], 0)
             narrow(cmp_f.at[1], s48.at[1], 0, 48)
             ws.start()
-        else:
-            for l in range(LEV):
-                n, j = R_WINDOW + 72 * b + 36 * l, token(l, SLAT)
-                stage_r[:, n : n + 36, :] = win_out[slot, :, j : j + 36, :]
-            narrow(stage_r, rs, *R_CUTS[b + 1][::2])
-            r_send(b + 1)
         keep(slot, SLAT, 9, col, WLON if b < 3 else SLON)
+
+    def window_n(b):
+        slot = b % 2
+        col = SLON + WLON * b
+        for l in range(LEV):
+            for i in range(SLAT):
+                j = token(l, SLAT + i)
+                win_in[slot, :, j : j + WLON, :] = fx[:, l, i, col : col + WLON, :]
+            j = token(l, 0)
+            if b < 3:
+                n = X_WINDOW + 72 * b + 36 * l
+                win_in[slot, :, j : j + 36, :] = stage_n[:, n : n + 36, :]
+            else:
+                for i in range(SLAT):
+                    n = SLON * (SLAT * l + i)
+                    jj = j + WLON * i
+                    win_in[slot, :, jj : jj + SLON, :] = stage_n[
+                        :, X_CORNER_E + n : X_CORNER_E + n + SLON, :
+                    ]
+                    win_in[slot, :, jj + SLON : jj + WLON, :] = cmp_f[1, :, n : n + SLON, :]
+        compute(2, slot)
+        own = WLON if b < 3 else SLON
+        for l in range(LEV):
+            for i in range(SLAT):
+                j = token(l, SLAT + i)
+                pf[:, l, i, col : col + own, :] = win_out[slot, :, j : j + own, :]
+        if b == 3:
+            pack(slot, SLAT, WLAT, SLON, SLON, cmp_f.at[0], 0)
+            narrow(cmp_f.at[0], s48.at[4], 0, 48)
+            wn.start()
 
     loads[C_WQKV].wait()
     loads[C_WOUT].wait()
     loads[C_B].wait()
-    for b in range(3):
-        window_m(b)
-
-    pl.when(inner)(lambda: pl.semaphore_wait(barrier, 6))
-    pl.when(jnp.logical_not(inner))(lambda: pl.semaphore_wait(barrier, 9))
-    for k in range(4):
-        x_send(k)
-    em.start()
-    es.start()
-    x_relay(0)
-    x_relay(1)
-    em.wait_recv()
-    widen(r80.at[0], cmp_f.at[0], 0, 80)
-    n = 0
-    for l in range(LEV):
-        for row in range(3, 9):
-            fx[:, l, row, 48 : 48 + SLON, :] = cmp_f[0, :, n : n + SLON, :]
-            n += SLON
-    window_m(3)
-    x_relay(2)
-    x_relay(3)
-
     def x_take(k):
         x_direct(k).wait_recv()
         x_other(k).wait_recv()
-        if k == 0:
-            corner.start()
         widen(xr, stage, *X_CUTS[k][::2])
 
+    def last_of_first_band():
+        em.wait_recv()
+        unpack_east(r80.at[0], 0, 3, 9, 80)
+        window_m(3)
+
+    def step_of_sends(k):
+        pl.when(early_send)(lambda: x_send(k))
+
+    window_m(0)
+    step_of_sends(2)
+    window_m(1)
+    pl.when(tail)(lambda: t_send(1))
+    step_of_sends(3)
+    x_relay(0)
+    window_m(2)
+    pl.when(tail)(lambda: t_send(2))
+    x_relay(1)
+    pl.when(early_send)(last_of_first_band)
+    pl.when(tail)(lambda: t_send(3))
+    x_relay(2)
+    x_relay(3)
+    t_relay(0, forward_first)
+
     x_take(0)
+    pl.when(early_send)(corner.start)
+    x_take(1)
+    window_s(0)
+    t_relay(1, forward_first)
+    x_take(2)
+    window_s(1)
+    t_relay(2, forward_first)
+    @pl.when(late_send)
+    def _():
+        greet_and_send()
+        corner.start()
+        r_copy(0).start()
+        r_copy(1).start()
+        x_send(2)
+        x_send(3)
+
+    x_take(3)
+    window_s(2)
+    t_relay(3, forward_first)
+    pl.when(late_send)(last_of_first_band)
     es.wait_recv()
-    widen(r48.at[0], cmp_f.at[0], 0, 48)
-    n = 0
-    for l in range(LEV):
-        for row in range(9, 12):
-            fx[:, l, row, 48 : 48 + SLON, :] = cmp_f[0, :, n : n + SLON, :]
-            n += SLON
+    unpack_east(r48.at[0], 0, 9, 12, 48)
     corner.wait_recv()
     widen(cor, cmp_f.at[1], 0, 48)
     window_s(3)
-    for b in range(3):
-        x_take(b + 1)
-        window_s(b)
-    r_relay(0)
+    t_relay(0, forward_last)
 
     loads[C_G].wait()
     loads[C_H].wait()
@@ -379,42 +486,109 @@
                 pf[:, l, row0 + i, col : col + width, :] = src[:, n : n + width, :]
                 n += width
 
-    wm.wait_recv()
-    widen(r80.at[1], cmp_f.at[0], 0, 80)
-    place_rows(cmp_f.at[0], 0, SLON, 3, WLAT, 0)
-    finish(3, 9)
-    r_relay(1)
-    ws.wait_recv()
-    widen(r48.at[1], cmp_f.at[1], 0, 48)
-    place_rows(cmp_f.at[1], 0, SLON, 9, SLAT, 0)
-    finish(9, 12)
-    r_relay(2)
-    r_relay(3)
-    diag.wait_recv()
-    widen(r48.at[2], cmp_f.at[1], 0, 48)
-    place_rows(cmp_f.at[1], 0, SLON, 0, SLAT, 0)
-    groups = [(36 * l + WLON * i + 72 * b + R_WINDOW, WLON, l, i, SLON + WLON * b)
-              for b in range(3) for l in range(LEV) for i in range(SLAT)]
-    groups += [(SLON * (SLAT * l + i), SLON, l, i, 42) for l in range(LEV) for i in range(SLAT)]
-    for k in range(4):
-        r_direct(k).wait_recv()
-        r_other(k).wait_recv()
-        a, _, b = R_CUTS[k]
-        widen(rr, stage, a, b)
-        for n, width, l, i, col in groups:
-            if a < n + width <= b:
-                pf[:, l, i, col : col + width, :] = stage[:, n : n + width, :]
+    def finish_own():
+        wm.wait_recv()
+        widen(r80.at[1], cmp_f.at[0], 0, 80)
+        place_rows(cmp_f.at[0], 0, SLON, 3, WLAT, 0)
+        finish(3, 9)
+        ws.wait_recv()
+        widen(r48.at[1], cmp_f.at[0], 0, 48)
+        place_rows(cmp_f.at[0], 0, SLON, 9, SLAT, 0)
+        finish(9, 12)
+
+    pl.when(not_head)(finish_own)
+
+    @pl.when(not_head)
+    def _():
+        diag.wait_recv()
+        widen(r48.at[2], cmp_f.at[1], 0, 48)
+        place_rows(cmp_f.at[1], 0, SLON, 0, SLAT, 0)
+        groups = [(36 * l + WLON * i + 72 * b, WLON, l, i, SLON + WLON * b)
+                  for b in range(3) for l in range(LEV) for i in range(SLAT)]
+        groups += [(R_CORNER + SLON * (SLAT * l + i), SLON, l, i, 42) for l in range(LEV) for i in range(SLAT)]
+        for k in range(4):
+            r_copy(k).wait_recv()
+            a, b = R_CUTS[k]
+            widen(rr, stage, a, b)
+            for n, width, l, i, col in groups:
+                if a < n + width <= b:
+                    pf[:, l, i, col : col + width, :] = stage[:, n : n + width, :]
+
+    @pl.when(head)
+    def _():
+        def t_take(k):
+            t_direct(k).wait_recv()
+            t_forward(k).wait_recv()
+            if k == 0:
+                corner_n.start()
+            widen(rr, stage_n, *X_CUTS[k][::2])
+
+        b_direct.wait_recv()
+        b_pair.start()
+        t_take(0)
+        t_relay(1, forward_last)
+        b_pair.wait_recv()
+        for g in range(HEADS + 1):
+            bt[g] = jnp.zeros((WT, 128), F32)
+        for src, side in ((br, core), (bp, 1 - core)):
+            bstage[...] = src[...].astype(F32)
+            for g in range(4):
+                bt[4 * side + g, 36:72, :] = bstage[HALF * g : HALF * g + 36, :]
+                bt[4 * side + g, 108:WT, :] = bstage[HALF * g + 36 : HALF * (g + 1), :]
+            for c in range(2):
+                @pl.when(side == c)
+                def _():
+                    bt[HEADS, 36 + 72 * c : 72 + 72 * c, :] = bstage[4 * HALF : 4 * HALF + 36, :]
+        at_pole = jnp.logical_and(south_half(0) != south_half(1), ilat == 0)
+        pole = jnp.where(at_pole, F32(-1e30), F32(0.0))
+        for h in range(HEADS):
+            rest = bt[HEADS][:, 16 * h : 16 * (h + 1)]
+            biasf[2, h // 2, WT * (h % 2) : WT * (h % 2 + 1), :] = (
+                jnp.concatenate([bt[h], rest], 1) + pole
+            )
+        en.wait_recv()
+        unpack_east(r48.at[3], 0, 0, 3, 48)
+        corner_n.wait_recv()
+        widen(corn, cmp_f.at[1], 0, 48)
+        t_relay(2, forward_last)
+        t_relay(3, forward_last)
+        window_n(3)
+        finish_own()
+        for b in range(3):
+            t_take(b + 1)
+            window_n(b)
+        wn.wait_recv()
+        widen(r48.at[4], cmp_f.at[1], 0, 48)
+        place_rows(cmp_f.at[1], 0, SLON, 0, SLAT, 0)
+
     finish(0, 3)
 
-    for copy in (em, es, corner, wm, ws, diag):
+    for copy in (em, es, corner, wm, ws):
         copy.wait_send()
     for k in range(4):
         x_direct(k).wait_send()
         x_other(k).wait_send()
-        r_direct(k).wait_send()
-        r_other(k).wait_send()
-        pl.when(tail)(x_forward(k).wait_send)
-        pl.when(head)(r_forward(k).wait_send)
+
+    @pl.when(not_tail)
+    def _():
+        diag.wait_send()
+        for k in range(4):
+            r_copy(k).wait_send()
+
+    @pl.when(tail)
+    def _():
+        b_direct.wait_send()
+        for k in range(4):
+            x_forward(k).wait_send()
+            t_direct(k).wait_send()
+            t_around(k).wait_send()
+
+    @pl.when(head)
+    def _():
+        for copy in (en, wn, corner_n, b_pair):
+            copy.wait_send()
+        for k in range(4):
+            t_forward(k).wait_send()
 
 
 def local_step(nlat, nlon, latent, w_qkv, w_out, b_out, norm_gain, norm_shift, earth_bias):
@@ -433,24 +607,31 @@
             pltpu.VMEM((1, D), F32),
             pltpu.VMEM((1, D), F32),
             pltpu.VMEM((2, HEADS, WT, WT), BF16),
-            pltpu.VMEM((2, HEADS // 2, 2 * WT, WT), F32),
+            pltpu.VMEM((3, HEADS // 2, 2 * WT, WT), F32),
             pltpu.VMEM((LT, LEV, 12, 64, 128), F32),
             pltpu.VMEM((LT, LEV, 12, 48, 128), F32),
             pltpu.VMEM((2, LT, WT, 128), F32),
             pltpu.VMEM((2, LT, WT, 128), F32),
             pltpu.VMEM((LT, 288, 128), F32),
+            pltpu.VMEM((LT, 288, 128), F32),
             pltpu.VMEM((LT, 256, 128), F32),
             pltpu.VMEM((288, D), BF16),
             pltpu.VMEM((288, D), BF16),
             pltpu.VMEM((288, D), BF16),
-            pltpu.VMEM((256, D), BF16),
-            pltpu.VMEM((256, D), BF16),
-            pltpu.VMEM((256, D), BF16),
+            pltpu.VMEM((288, D), BF16),
+            pltpu.VMEM((288, D), BF16),
+            pltpu.VMEM((288, D), BF16),
+            pltpu.VMEM((HEADS + 1, WT, 128), F32),
+            pltpu.VMEM((B_ROWS, 128), F32),
+            pltpu.VMEM((B_ROWS, 128), BF16),
+            pltpu.VMEM((B_ROWS, 128), BF16),
+            pltpu.VMEM((B_ROWS, 128), BF16),
             pltpu.VMEM((2, LT, 80, 128), F32),
             pltpu.VMEM((2, 80, D), BF16),
-            pltpu.VMEM((3, 48, D), BF16),
+            pltpu.VMEM((5, 48, D), BF16),
             pltpu.VMEM((2, 80, D), BF16),
-            pltpu.VMEM((3, 48, D), BF16),
+            pltpu.VMEM((5, 48, D), BF16),
+            pltpu.VMEM((48, D), BF16),
             pltpu.VMEM((48, D), BF16),
             pltpu.SemaphoreType.DMA((9,)),
             pltpu.SemaphoreType.DMA((COPIES,)),

time: 41.4 us -> 33.4 us (0.81)
  Pallas kernels: 40.2 us -> 32.2 us
    pallas_call x1, Pallas kernels: 40.2 us -> 32.2 us  [local_step(): pl.pallas_call(functools.partial(kernel, nlat, nlon), out_shape=pltpu.VME...]
where the time goes in v3:
time: 33.4 us; the launch traced here: 33.3 us
  Pallas kernels  32.2 us (96%)
  local copies, waits for them, and re-layouts  1.02 us (3%)
    pallas_call x1, Pallas kernels, local_step(): pl.pallas_call(functools.partial(kernel, nlat, nlon), out_shape=pltpu.VME...  32.2 us
    unnamed x1, local copies, waits for them, and re-layouts  1.02 us

profile of v3, /device:TPU:1, one launch (start us, length us, event | category | flops | bytes accessed | tf_op | source)
XLA Modules:
  0.0 33.3 jit_solution(3808760964992526942)
XLA Ops:
  0.0 32.2 %swin_window_attention.1 = bf16[2,12,48,512]{3,2,1,0:T(8,128)(2,1)S(1)} custom-call(bf16[2,12,48,512]{3,2,1,0:T(8,128)(2,1)} %lat_h.1, bf16[512,1536]{1,0:T(8,128)(2,1)} %wqkv_h.1, bf16[512,512]{1,0:T(8,128)(2,1)} %wout_h.1, f32[1,512]{1,0:T(1,128)} %bitcast.3, f32[1,512]{1,0:T(1,128)} %bitcast.4, f32[1,512]{1,0:T(1,128)} %bitcast.5, ...), custom_call_target="tpu_custom_call" | custom-call | tf_op jit(solution)/shard_map/swin_window_attention/pallas_call | solution.py:597
  32.2 1.0 %copy.9 = bf16[2,12,48,512]{3,2,1,0:T(8,128)(2,1)} copy(bf16[2,12,48,512]{3,2,1,0:T(8,128)(2,1)S(1)} %swin_window_attention.1) | data formatting | bytes 2359296

commit v4 on v3

--- a/solution.py
+++ b/solution.py
@@ -34,12 +34,13 @@
 R_CORNER = 216
 B_ROWS = 336
 HALF = WT // 2
+HALF_ROWS = 80
 
 
 def kernel(
     nlat, nlon,
     lat_h, wqkv_h, wout_h, b_h, gain_h, shift_h, bias_h, out_v,
-    lat_v, wqkv, wout, b_out, gain, shift, bias_v, biasf, fx, pf, win_in, win_out,
+    lat_v, wqkv, wout, b_out, gain, shift, bias_v, biasf, bias_n, fx, pf, win_in, win_q, win_out,
     stage, stage_n, stage_r, xs, xr, xrelay, rs, rr, rrelay, bt, bstage, bs, br, bp,
     cmp_f, s80, s48, r80, r48, cor, corn,
     lsem, ssem, rsem,
@@ -249,10 +250,10 @@
     def greet_and_send():
         pl.when(inner)(lambda: pl.semaphore_wait(barrier, 6))
         pl.when(head)(lambda: pl.semaphore_wait(barrier, 9))
-        x_send(0)
         em.start()
         es.start()
         pl.when(head)(en.start)
+        x_send(0)
         x_send(1)
 
     pl.when(early_send)(greet_and_send)
@@ -275,21 +276,28 @@
     scale0 = jnp.where(first, F32(0.125), F32(0.0))
     scale1 = jnp.where(first, F32(0.0), F32(0.125))
 
-    def attend(r, x):
-        qkv = jnp.dot(x, wqkv[...], preferred_element_type=F32)
+    def attend(bias, x, queries=None):
+        if queries is None:
+            size = WT
+            qkv = jnp.dot(x, wqkv[...], preferred_element_type=F32)
+            q, kv = qkv[:, :D], qkv[:, D:]
+        else:
+            size = queries.shape[0]
+            q = jnp.dot(queries, wqkv[:, :D], preferred_element_type=F32)
+            kv = jnp.dot(x, wqkv[:, D:], preferred_element_type=F32)
         parts = []
         for p in range(HEADS // 2):
-            qf = qkv[:, 128 * p : 128 * (p + 1)]
-            kp = qkv[:, D + 128 * p : D + 128 * (p + 1)].astype(BF16)
-            vp = qkv[:, 2 * D + 128 * p : 2 * D + 128 * (p + 1)].astype(BF16)
+            qf = q[:, 128 * p : 128 * (p + 1)]
+            kp = kv[:, 128 * p : 128 * (p + 1)].astype(BF16)
+            vp = kv[:, D + 128 * p : D + 128 * (p + 1)].astype(BF16)
             q2 = jnp.concatenate([(qf * scale0).astype(BF16), (qf * scale1).astype(BF16)], 0)
             s = lax.dot_general(q2, kp, (((1,), (1,)), ((), ())), preferred_element_type=F32)
-            s = s + biasf[r, p]
+            s = s + bias[p]
             e = jnp.exp(s - jnp.max(s, axis=-1, keepdims=True)).astype(BF16)
             vx = jnp.concatenate([vp, jnp.ones((WT, 128), BF16)], 1)
             o = jnp.dot(e, vx, preferred_element_type=F32)
-            num = jnp.where(first, o[:WT, :128], o[WT:, :128])
-            den = jnp.where(first, o[:WT, 128:], o[WT:, 128:])
+            num = jnp.where(first, o[:size, :128], o[size:, :128])
+            den = jnp.where(first, o[:size, 128:], o[size:, 128:])
             parts.append((num / den).astype(BF16))
         att = jnp.concatenate(parts, 1)
         proj = jnp.dot(att, wout[...], preferred_element_type=F32) + b_out[...]
@@ -300,7 +308,7 @@
 
     def compute(r, slot):
         x = jnp.concatenate([win_in[slot, t].astype(BF16) for t in range(LT)], 1)
-        proj = attend(r, x)
+        proj = attend(biasf.at[r], x)
         for t in range(LT):
             win_out[slot, t] = proj[:, 128 * t : 128 * (t + 1)]
 
@@ -384,7 +392,10 @@
         for l in range(LEV):
             for i in range(SLAT):
                 j = token(l, SLAT + i)
-                win_in[slot, :, j : j + WLON, :] = fx[:, l, i, col : col + WLON, :]
+                piece = fx[:, l, i, col : col + WLON, :]
+                win_in[slot, :, j : j + WLON, :] = piece
+                n = 36 * l + WLON * i
+                win_q[slot, :, n : n + WLON, :] = piece
             j = token(l, 0)
             if b < 3:
                 n = X_WINDOW + 72 * b + 36 * l
@@ -397,14 +408,21 @@
                         :, X_CORNER_E + n : X_CORNER_E + n + SLON, :
                     ]
                     win_in[slot, :, jj + SLON : jj + WLON, :] = cmp_f[1, :, n : n + SLON, :]
-        compute(2, slot)
+        win_q[slot, :, HALF:HALF_ROWS, :] = jnp.zeros((LT, HALF_ROWS - HALF, 128), F32)
+        x = jnp.concatenate([win_in[slot, t].astype(BF16) for t in range(LT)], 1)
+        queries = jnp.concatenate([win_q[slot, t].astype(BF16) for t in range(LT)], 1)
+        proj = attend(bias_n, x, queries)
+        for t in range(LT):
+            win_out[slot, t, 0:HALF_ROWS] = proj[:, 128 * t : 128 * (t + 1)]
         own = WLON if b < 3 else SLON
         for l in range(LEV):
             for i in range(SLAT):
-                j = token(l, SLAT + i)
+                j = 36 * l + WLON * i
                 pf[:, l, i, col : col + own, :] = win_out[slot, :, j : j + own, :]
+                if b == 3:
+                    n = SLON * (SLAT * l + i)
+                    cmp_f[0, :, n : n + SLON, :] = win_out[slot, :, j + SLON : j + WLON, :]
         if b == 3:
-            pack(slot, SLAT, WLAT, SLON, SLON, cmp_f.at[0], 0)
             narrow(cmp_f.at[0], s48.at[4], 0, 48)
             wn.start()
 
@@ -437,6 +455,7 @@
     pl.when(tail)(lambda: t_send(3))
     x_relay(2)
     x_relay(3)
+
     t_relay(0, forward_first)
 
     x_take(0)
@@ -465,7 +484,6 @@
     corner.wait_recv()
     widen(cor, cmp_f.at[1], 0, 48)
     window_s(3)
-    t_relay(0, forward_last)
 
     loads[C_G].wait()
     loads[C_H].wait()
@@ -496,6 +514,7 @@
         place_rows(cmp_f.at[0], 0, SLON, 9, SLAT, 0)
         finish(9, 12)
 
+    t_relay(0, forward_last)
     pl.when(not_head)(finish_own)
 
     @pl.when(not_head)
@@ -528,24 +547,23 @@
         t_take(0)
         t_relay(1, forward_last)
         b_pair.wait_recv()
-        for g in range(HEADS + 1):
-            bt[g] = jnp.zeros((WT, 128), F32)
         for src, side in ((br, core), (bp, 1 - core)):
             bstage[...] = src[...].astype(F32)
             for g in range(4):
-                bt[4 * side + g, 36:72, :] = bstage[HALF * g : HALF * g + 36, :]
-                bt[4 * side + g, 108:WT, :] = bstage[HALF * g + 36 : HALF * (g + 1), :]
+                bt[4 * side + g, 0:HALF, :] = bstage[HALF * g : HALF * (g + 1), :]
             for c in range(2):
                 @pl.when(side == c)
                 def _():
-                    bt[HEADS, 36 + 72 * c : 72 + 72 * c, :] = bstage[4 * HALF : 4 * HALF + 36, :]
-        at_pole = jnp.logical_and(south_half(0) != south_half(1), ilat == 0)
+                    bt[HEADS, 36 * c : 36 * (c + 1), :] = bstage[4 * HALF : 4 * HALF + 36, :]
+        key = lax.broadcasted_iota(jnp.int32, (HALF, WT), 1)
+        south_key = jnp.logical_or(jnp.logical_and(key >= 36, key < 72), key >= 108)
+        at_pole = jnp.logical_and(jnp.logical_not(south_key), ilat == 0)
         pole = jnp.where(at_pole, F32(-1e30), F32(0.0))
         for h in range(HEADS):
-            rest = bt[HEADS][:, 16 * h : 16 * (h + 1)]
-            biasf[2, h // 2, WT * (h % 2) : WT * (h % 2 + 1), :] = (
-                jnp.concatenate([bt[h], rest], 1) + pole
-            )
+            n = HALF_ROWS * (h % 2)
+            rest = bt[HEADS, 0:HALF, :][:, 16 * h : 16 * (h + 1)]
+            bias_n[h // 2, n : n + HALF, :] = jnp.concatenate([bt[h, 0:HALF, :], rest], 1) + pole
+            bias_n[h // 2, n + HALF : n + HALF_ROWS, :] = jnp.zeros((HALF_ROWS - HALF, WT), F32)
         en.wait_recv()
         unpack_east(r48.at[3], 0, 0, 3, 48)
         corner_n.wait_recv()
@@ -607,10 +625,12 @@
             pltpu.VMEM((1, D), F32),
             pltpu.VMEM((1, D), F32),
             pltpu.VMEM((2, HEADS, WT, WT), BF16),
-            pltpu.VMEM((3, HEADS // 2, 2 * WT, WT), F32),
+            pltpu.VMEM((2, HEADS // 2, 2 * WT, WT), F32),
+            pltpu.VMEM((HEADS // 2, 2 * HALF_ROWS, WT), F32),
             pltpu.VMEM((LT, LEV, 12, 64, 128), F32),
             pltpu.VMEM((LT, LEV, 12, 48, 128), F32),
             pltpu.VMEM((2, LT, WT, 128), F32),
+            pltpu.VMEM((2, LT, HALF_ROWS, 128), F32),
             pltpu.VMEM((2, LT, WT, 128), F32),
             pltpu.VMEM((LT, 288, 128), F32),
             pltpu.VMEM((LT, 288, 128), F32),

time: 33.4 us -> 32.9 us (0.985)
  Pallas kernels: 32.2 us -> 31.7 us
    pallas_call x1, Pallas kernels: 32.2 us -> 31.7 us  [local_step(): pl.pallas_call(functools.partial(kernel, nlat, nlon), out_shape=pltpu.VME...]
where the time goes in v4:
time: 32.9 us; the launch traced here: 32.8 us
  Pallas kernels  31.7 us (96%)
  local copies, waits for them, and re-layouts  1.02 us (3%)
    pallas_call x1, Pallas kernels, local_step(): pl.pallas_call(functools.partial(kernel, nlat, nlon), out_shape=pltpu.VME...  31.7 us
    unnamed x1, local copies, waits for them, and re-layouts  1.02 us

profile of v4, /device:TPU:1, one launch (start us, length us, event | category | flops | bytes accessed | tf_op | source)
XLA Modules:
  0.0 32.8 jit_solution(2689428957533764503)
XLA Ops:
  0.0 31.7 %swin_window_attention.1 = bf16[2,12,48,512]{3,2,1,0:T(8,128)(2,1)S(1)} custom-call(bf16[2,12,48,512]{3,2,1,0:T(8,128)(2,1)} %lat_h.1, bf16[512,1536]{1,0:T(8,128)(2,1)} %wqkv_h.1, bf16[512,512]{1,0:T(8,128)(2,1)} %wout_h.1, f32[1,512]{1,0:T(1,128)} %bitcast.3, f32[1,512]{1,0:T(1,128)} %bitcast.4, f32[1,512]{1,0:T(1,128)} %bitcast.5, ...), custom_call_target="tpu_custom_call" | custom-call | tf_op jit(solution)/shard_map/swin_window_attention/pallas_call | solution.py:615
  31.8 1.0 %copy.9 = bf16[2,12,48,512]{3,2,1,0:T(8,128)(2,1)} copy(bf16[2,12,48,512]{3,2,1,0:T(8,128)(2,1)S(1)} %swin_window_attention.1) | data formatting | bytes 2359296
